TPU v7x, 32 devices: a whole 2x2x4 slice. The times are simulated.
32 devices in a mesh: group: 2 (over y), dom: 4 (over z), row: 4 (over x, core).
Axes of the slice: x: 2, y: 2, z: 4, core: 2. Of those that a mesh axis runs over, the one named last changes fastest.
Arguments:
- state: bfloat16 [8, 16, 10752], P(('group', 'dom'), 'row'), parts along dimension 0, may hold values from -6 to 6
- prev_pred: bfloat16 [8, 16, 10752], P(('group', 'dom'), 'row'), parts along dimension 0, may hold values from -6 to 6
- ancestors: int32 [8], P('group'), parts along dimension 0, may hold values from 0 to 3, as said below
- timestep: int32 [2], P('group'), parts along dimension 0, may hold values from 50 to 949
- w_in: bfloat16 [168, 256], replicated, may hold values from -0.5 to 0.5
- w_time: bfloat16 [256, 256], replicated, may hold values from -0.375 to 0.375
- w_qkv: bfloat16 [2, 256, 768], replicated, may hold values from -0.375 to 0.375
- w_attn_out: bfloat16 [2, 256, 256], replicated, may hold values from -0.375 to 0.375
- w_up: bfloat16 [2, 256, 1024], replicated, may hold values from -0.375 to 0.375
- w_down: bfloat16 [2, 1024, 256], replicated, may hold values from -0.1875 to 0.1875
- w_out: bfloat16 [256, 84], replicated, may hold values from -0.375 to 0.375
Outputs:
- new_state: bfloat16 [8, 16, 10752], P(('group', 'dom'), 'row'), parts along dimension 0
- new_pred: bfloat16 [8, 16, 10752], P(('group', 'dom'), 'row'), parts along dimension 0
There are 2 independent parts, one for each index of `group`. A program takes and returns all parts, laid end to end along the dimension named above; an argument that names none is the same for every part. Nothing has to cross between parts.
Inputs may be any that keep to these rules, and one draw needn't show every extreme that they name: ancestors[j] is the particle of the same group whose state particle j takes; the list never falls.
All inputs are finite; a program needn't handle non-finite values.
Results may differ from a plain program's by a relative error of at most 0.018.
Values may be sent and summed in bfloat16 or wider, within the bound.
No kernel may reach another device: no remote copies, remote signals or barrier semaphores. Data moves between devices by JAX's collectives and lax.ppermute only.
A program may use at most 64 MiB of HBM per device.

v0:
```python
import math

import jax
import jax.numpy as jnp
from jax import lax
from jax.sharding import PartitionSpec as P

D = 256
HEADS = 8
CH = 84
COLS = 128
STEPS = 1000
STRIDE = 20


def rms_round(values_in):
    widened = values_in.astype(jnp.float32)
    scaled = widened * lax.rsqrt(jnp.mean(widened * widened, axis=-1, keepdims=True) + 1e-06)
    return scaled.astype(jnp.bfloat16)


def unit_rows(values_in):
    return values_in * lax.rsqrt(jnp.mean(values_in * values_in, axis=-1, keepdims=True) + 1e-06)


def rotate(values_in, span_len):
    half_size = values_in.shape[-1] // 2
    places = jnp.arange(span_len, dtype=jnp.float32)
    rates = jnp.exp(-math.log(10000.0) * jnp.arange(half_size, dtype=jnp.float32) / half_size)
    angles = places[:, None] * rates[None, :]
    cos_part = jnp.cos(angles)[:, None, None, :]
    sin_part = jnp.sin(angles)[:, None, None, :]
    leading = values_in[..., :half_size]
    trailing = values_in[..., half_size:]
    return jnp.concatenate(
        [leading * cos_part - trailing * sin_part, leading * sin_part + trailing * cos_part],
        axis=-1,
    )


def attend(normed, weight_qkv, weight_out):
    batch_size, span_len, side_len, model_width = normed.shape
    head_size = model_width // HEADS
    joined = jnp.dot(normed, weight_qkv, preferred_element_type=jnp.float32)
    queries = unit_rows(joined[..., :model_width]).reshape(
        batch_size, span_len, side_len, HEADS, head_size
    )
    key_rows = unit_rows(joined[..., model_width : 2 * model_width]).reshape(
        batch_size, span_len, side_len, HEADS, head_size
    )
    values = (
        joined[..., 2 * model_width :]
        .astype(jnp.bfloat16)
        .reshape(batch_size, span_len, side_len, HEADS, head_size)
    )
    queries = rotate(queries, span_len).astype(jnp.bfloat16)
    key_rows = rotate(key_rows, span_len).astype(jnp.bfloat16)
    scores = jnp.einsum(
        "blmhe,bkmhe->bmhlk", queries, key_rows, preferred_element_type=jnp.float32
    ) / math.sqrt(head_size)
    weights = jnp.exp(scores)
    shares = (weights / jnp.sum(weights, axis=-1, keepdims=True)).astype(jnp.bfloat16)
    mixture = jnp.einsum("bmhlk,bkmhe->blmhe", shares, values, preferred_element_type=jnp.float32)
    mixture = mixture.astype(jnp.bfloat16).reshape(batch_size, span_len, side_len, model_width)
    return jnp.dot(mixture, weight_out, preferred_element_type=jnp.float32)


def mix_tokens(hidden, weight_qkv, weight_out):
    return (hidden.astype(jnp.float32) + attend(rms_round(hidden), weight_qkv, weight_out)).astype(
        jnp.bfloat16
    )


def feed_forward(hidden, weight_up, weight_down):
    lifted = jnp.dot(rms_round(hidden), weight_up, preferred_element_type=jnp.float32)
    gated = jax.nn.gelu(lifted, approximate=True).astype(jnp.bfloat16)
    return (
        hidden.astype(jnp.float32) + jnp.dot(gated, weight_down, preferred_element_type=jnp.float32)
    ).astype(jnp.bfloat16)


def level(moment):
    cosine = jnp.cos((moment / STEPS + 0.008) / 1.008 * math.pi / 2.0)
    return cosine * cosine


def time_vector(timestep, w_time):
    moment = timestep[0].astype(jnp.float32)
    half_size = w_time.shape[0] // 2
    rates = jnp.exp(-math.log(10000.0) * jnp.arange(half_size, dtype=jnp.float32) / half_size)
    embedded = jnp.concatenate([jnp.sin(moment * rates), jnp.cos(moment * rates)])
    return jnp.dot(embedded, w_time.astype(jnp.float32), precision=lax.Precision.HIGHEST)


def network(state_rows, prev_rows, offset_vec, w_in, w_qkv, w_attn_out, w_up, w_down, w_out):
    part_count, row_count, flat_width = state_rows.shape
    joined = jnp.concatenate(
        [
            state_rows.reshape(part_count, row_count, COLS, CH),
            prev_rows.reshape(part_count, row_count, COLS, CH),
        ],
        axis=-1,
    )
    hidden = (jnp.dot(joined, w_in, preferred_element_type=jnp.float32) + offset_vec).astype(
        jnp.bfloat16
    )
    hidden = hidden.reshape(part_count * row_count, COLS, 1, D)
    hidden = mix_tokens(hidden, w_qkv[0], w_attn_out[0])
    hidden = feed_forward(hidden, w_up[0], w_down[0])
    hidden = hidden.reshape(part_count, row_count, COLS, D)
    columns = lax.all_to_all(hidden, "row", split_axis=2, concat_axis=1, tiled=True)
    columns = mix_tokens(columns, w_qkv[1], w_attn_out[1])
    hidden = lax.all_to_all(columns, "row", split_axis=1, concat_axis=2, tiled=True)
    hidden = feed_forward(hidden, w_up[1], w_down[1])
    predicted = jnp.dot(rms_round(hidden), w_out, preferred_element_type=jnp.float32).astype(
        jnp.bfloat16
    )
    predicted = predicted.reshape(part_count, row_count, flat_width)
    return predicted


def per_device(
    state, prev_pred, ancestors, timestep, w_in, w_time, w_qkv, w_attn_out, w_up, w_down, w_out
):
    offset_vec = time_vector(timestep, w_time)
    moment = timestep[0].astype(jnp.float32)
    level_now = level(moment)
    level_next = level(moment - STRIDE)
    chosen_state = lax.all_to_all(
        jnp.take(
            lax.all_to_all(state, "dom", split_axis=2, concat_axis=0, tiled=True), ancestors, axis=0
        ),
        "dom",
        split_axis=0,
        concat_axis=2,
        tiled=True,
    )
    own_pred = network(state, prev_pred, offset_vec, w_in, w_qkv, w_attn_out, w_up, w_down, w_out)
    predicted = lax.all_to_all(
        jnp.take(
            lax.all_to_all(own_pred, "dom", split_axis=2, concat_axis=0, tiled=True),
            ancestors,
            axis=0,
        ),
        "dom",
        split_axis=0,
        concat_axis=2,
        tiled=True,
    )
    widened = chosen_state.astype(jnp.float32)
    pred_wide = predicted.astype(jnp.float32)
    noise_est = (widened - jnp.sqrt(level_now) * pred_wide) / jnp.sqrt(1.0 - level_now)
    updated = (jnp.sqrt(level_next) * pred_wide + jnp.sqrt(1.0 - level_next) * noise_est).astype(
        jnp.bfloat16
    )
    return (updated, predicted)


def solution(mesh):
    in_specs = (
        P(("group", "dom"), "row", None),
        P(("group", "dom"), "row", None),
        P("group"),
        P("group"),
        P(),
        P(),
        P(),
        P(),
        P(),
        P(),
        P(),
    )
    out_specs = (P(("group", "dom"), "row", None), P(("group", "dom"), "row", None))
    return jax.shard_map(
        per_device, mesh=mesh, in_specs=in_specs, out_specs=out_specs, check_vma=False
    )
```

profile of v0, /device:TPU:0, one launch (start us, length us, event | category | flops | bytes accessed | tf_op | source)
XLA Modules:
  0.0 268.8 jit_solution(5302937269611741926)
XLA Ops:
  9.7 2.1 fusion.32
  12.7 4.4 %all-to-all-start = ((bf16[1,4,128,256]{3,1,0,2:T(4,128)(2,1)}), bf16[1,4,128,256]{3,1,0,2:T(4,128)(2,1)S(1)}, u32[]{:S(2)}, u32[]{:S(2)}) async-start(bf16[1,4,128,256]{3,1,0,2:T(4,128)(2,1)} %copy.77), calls=%async_computation | async-start | bytes 524288 | tf_op jit(solution)/shard_map/all_to_all | solution.py:111
  17.1 8.8 %copy.92 = bf16[1,4,10752]{1,0,2:T(2,128)(2,1)} copy(bf16[1,4,10752]{2,1,0:T(4,128)(2,1)S(1)} %copy-done.5) | data formatting | bytes 172032 | tf_op args[0]
  26.4 58.9 %reduce.19 = bf16[10752,4]{1,0:T(8,128)(2,1)S(1)} reduce(bf16[10752,1,4]{2,1,0:T(2,128)(2,1)} %bitcast.158, bf16[]{:T(256)} %broadcast.323), dimensions={1}, to_apply=%bitcast.139.reduce_sub_computation | reduce | bytes 172034
  85.3 5.9 %reshape.588 = bf16[4,2,5376]{2,1,0:T(2,128)(2,1)} reshape(bf16[10752,4]{1,0:T(8,128)(2,1)S(1)} %reduce.19) | data formatting | bytes 172032
  95.4 1.8 reshape.541
  97.2 1.8 reshape.540
  99.1 2.9 %fusion.121 = (f32[1,16,32,8,16]{4,3,2,1,0:T(8,128)S(1)}, f32[1,16,32,8,16]{4,3,2,1,0:T(8,128)S(1)}) fusion(f32[1,16,32,8,32]{4,3,2,1,0:T(8,128)} %reshape.540), kind=kLoop, calls=%fused_computation.183 | loop fusion | bytes 1048576 | tf_op jit(solution)/shard_map/slice | solution.py:33
  102.7 4.9 %fusion.35 = (bf16[16,32,8,16]{3,0,2,1:T(8,128)(2,1)S(1)}, bf16[16,32,8,16]{3,0,2,1:T(8,128)(2,1)S(1)}, bf16[16,32,8,16]{3,0,2,1:T(8,128)(2,1)S(1)}, bf16[16,32,8,16]{3,0,2,1:T(8,128)(2,1)S(1)}) fusion(f32[1,16,32,8,16]{4,3,2,1,0:T(8,128)S(1)} %get-tuple-element.12, f32[1,16,32,8,16]{4,3,2,1,0:T(8,128)S(1)} %get-tuple-element.11, ...), kind=kLoop, calls=%fused_computation.55 | loop fusion | flops 1048576 | bytes 1574912 | tf_op jit(solution)/shard_map/concatenate | solution.py:35
  112.3 3.4 %all-to-all-start.1 = ((bf16[1,16,32,256]{3,2,0,1:T(8,128)(2,1)}), bf16[1,16,32,256]{3,2,0,1:T(8,128)(2,1)S(1)}, u32[]{:S(2)}, u32[]{:S(2)}) async-start(bf16[1,16,32,256]{3,2,0,1:T(8,128)(2,1)} %fusion.31), calls=%async_computation.1 | async-start | bytes 524288 | tf_op jit(solution)/shard_map/all_to_all | solution.py:113
  115.7 6.0 %all-to-all-done.1 = bf16[1,16,32,256]{3,2,0,1:T(8,128)(2,1)S(1)} async-done(((bf16[1,16,32,256]{3,2,0,1:T(8,128)(2,1)}), bf16[1,16,32,256]{3,2,0,1:T(8,128)(2,1)S(1)}, u32[]{:S(2)}, u32[]{:S(2)}) %all-to-all-start.1) | async-done | bytes 262176 | tf_op jit(solution)/shard_map/all_to_all | solution.py:113
  121.7 5.7 %all-to-all-start.4 = ((bf16[4,2,5376]{2,1,0:T(2,128)(2,1)}), bf16[4,2,5376]{2,1,0:T(2,128)(2,1)S(1)}, u32[]{:S(2)}, u32[]{:S(2)}) async-start(bf16[4,2,5376]{2,1,0:T(2,128)(2,1)} %reshape.588), calls=%async_computation.4 | async-start | bytes 172032 | tf_op jit(solution)/shard_map/all_to_all | solution.py:131
  127.9 2.3 multiply_reduce_fusion
  130.8 8.8 %copy.89 = bf16[1,4,10752]{1,0,2:T(2,128)(2,1)} copy(bf16[1,4,10752]{2,1,0:T(4,128)(2,1)S(1)} %reshape.543) | data formatting | bytes 172032 | tf_op jit(solution)/shard_map/reshape | solution.py:118
  139.6 58.9 %reduce.20 = bf16[10752,4]{1,0:T(8,128)(2,1)S(1)} reduce(bf16[10752,1,4]{2,1,0:T(2,128)(2,1)} %bitcast.159, bf16[]{:T(256)} %broadcast.323), dimensions={1}, to_apply=%bitcast.137.reduce_sub_computation | reduce | bytes 172034
  198.5 5.9 %reshape.586 = bf16[4,2,5376]{2,1,0:T(2,128)(2,1)} reshape(bf16[10752,4]{1,0:T(8,128)(2,1)S(1)} %reduce.20) | data formatting | bytes 172032
  204.3 5.4 %all-to-all-start.2 = ((bf16[4,2,5376]{2,1,0:T(2,128)(2,1)}), bf16[4,2,5376]{2,1,0:T(2,128)(2,1)S(1)}, u32[]{:S(2)}, u32[]{:S(2)}) async-start(bf16[4,2,5376]{2,1,0:T(2,128)(2,1)} %reshape.586), calls=%async_computation.2 | async-start | bytes 172032 | tf_op jit(solution)/shard_map/all_to_all | solution.py:141
  209.8 7.2 %reshape.589 = bf16[10752,1,4]{2,1,0:T(2,128)(2,1)} reshape(bf16[4,2,5376]{2,1,0:T(2,128)(2,1)S(1)} %all-to-all-done.4) | data formatting | bytes 172032
  217.0 10.4 %copy.93 = bf16[1,4,10752]{2,1,0:T(4,128)(2,1)S(1)} copy(bf16[1,4,10752]{1,0,2:T(2,128)(2,1)} %bitcast.160) | data formatting | bytes 172032 | tf_op jit(solution)/shard_map/all_to_all | solution.py:131
  228.1 7.2 %reshape.587 = bf16[10752,1,4]{2,1,0:T(2,128)(2,1)} reshape(bf16[4,2,5376]{2,1,0:T(2,128)(2,1)S(1)} %all-to-all-done.2) | data formatting | bytes 172032
  235.3 10.5 %copy.90 = bf16[1,4,10752]{2,1,0:T(4,128)(2,1)S(1)} copy(bf16[1,4,10752]{1,0,2:T(2,128)(2,1)} %bitcast.161) | data formatting | bytes 172032 | tf_op jit(solution)/shard_map/all_to_all | solution.py:141
  247.2 10.7 %all_to_all.81 = bf16[4,4,2688]{2,1,0:T(4,128)(2,1)S(1)} all-to-all(bf16[4,4,2688]{2,1,0:T(4,128)(2,1)S(1)} %get-tuple-element.28), channel_id=1, replica_groups=mesh['group'=2,'dom'=4,'row'=4] {'dom'}, dimensions={0} | all-to-all | bytes 172032 | tf_op jit(solution)/shard_map/all_to_all | solution.py:139
  257.8 3.3 %all-to-all-start.5 = ((bf16[4,4,2688]{2,1,0:T(4,128)(2,1)}), bf16[4,4,2688]{2,1,0:T(4,128)(2,1)S(1)}, u32[]{:S(2)}, u32[]{:S(2)}) async-start(bf16[4,4,2688]{2,1,0:T(4,128)(2,1)} %get-tuple-element.27), calls=%async_computation.5 | async-start | bytes 172032 | tf_op jit(solution)/shard_map/all_to_all | solution.py:129
  261.5 5.4 %all-to-all-done.5 = bf16[4,4,2688]{2,1,0:T(4,128)(2,1)S(1)} async-done(((bf16[4,4,2688]{2,1,0:T(4,128)(2,1)}), bf16[4,4,2688]{2,1,0:T(4,128)(2,1)S(1)}, u32[]{:S(2)}, u32[]{:S(2)}) %all-to-all-start.5) | async-done | bytes 86048 | tf_op jit(solution)/shard_map/all_to_all | solution.py:129
  (86 shorter events, 23.6 us)
Async XLA Ops:
  0.6 3.8 %copy-start = (bf16[256,256]{1,0:T(8,128)(2,1)S(1)}, bf16[256,256]{1,0:T(8,128)(2,1)}, u32[]{:S(2)}) copy-start(bf16[256,256]{1,0:T(8,128)(2,1)} %param.18) | copy-start | bytes 393220
  0.6 5.3 %copy-start.3 = (bf16[2,256,768]{2,1,0:T(8,128)(2,1)S(1)}, bf16[2,256,768]{2,1,0:T(8,128)(2,1)}, u32[]{:S(2)}) copy-start(bf16[2,256,768]{2,1,0:T(8,128)(2,1)} %param.19) | copy-start | bytes 2359300
  8.3 1.0 copy-start.6
  8.4 1.3 copy-start.8
  9.7 7.4 %copy-start.5 = (bf16[1,4,10752]{2,1,0:T(4,128)(2,1)S(1)}, bf16[1,4,10752]{2,1,0:T(4,128)(2,1)}, u32[]{:S(2)}) copy-start(bf16[1,4,10752]{2,1,0:T(4,128)(2,1)} %param.13) | copy-start | bytes 258052
  12.7 78.5 %all-to-all-start = ((bf16[1,4,128,256]{3,1,0,2:T(4,128)(2,1)}), bf16[1,4,128,256]{3,1,0,2:T(4,128)(2,1)S(1)}, u32[]{:S(2)}, u32[]{:S(2)}) async-start(bf16[1,4,128,256]{3,1,0,2:T(4,128)(2,1)} %copy.77), calls=%async_computation | async-start | bytes 524288 | tf_op jit(solution)/shard_map/all_to_all | solution.py:111
  91.2 1.1 copy-start.4
  107.6 1.7 copy-start.2
  110.4 5.3 %copy-start.9 = (s32[4]{0:T(128)S(1)}, s32[4]{0:T(128)}, u32[]{:S(2)}) copy-start(s32[4]{0:T(128)} %param.15) | copy-start | bytes 52
  112.3 9.4 %all-to-all-start.1 = ((bf16[1,16,32,256]{3,2,0,1:T(8,128)(2,1)}), bf16[1,16,32,256]{3,2,0,1:T(8,128)(2,1)S(1)}, u32[]{:S(2)}, u32[]{:S(2)}) async-start(bf16[1,16,32,256]{3,2,0,1:T(8,128)(2,1)} %fusion.31), calls=%async_computation.1 | async-start | bytes 524288 | tf_op jit(solution)/shard_map/all_to_all | solution.py:113
  121.7 82.6 %all-to-all-start.4 = ((bf16[4,2,5376]{2,1,0:T(2,128)(2,1)}), bf16[4,2,5376]{2,1,0:T(2,128)(2,1)S(1)}, u32[]{:S(2)}, u32[]{:S(2)}) async-start(bf16[4,2,5376]{2,1,0:T(2,128)(2,1)} %reshape.588), calls=%async_computation.4 | async-start | bytes 172032 | tf_op jit(solution)/shard_map/all_to_all | solution.py:131
  127.9 2.3 copy-start.7
  204.3 23.7 %all-to-all-start.2 = ((bf16[4,2,5376]{2,1,0:T(2,128)(2,1)}), bf16[4,2,5376]{2,1,0:T(2,128)(2,1)S(1)}, u32[]{:S(2)}, u32[]{:S(2)}) async-start(bf16[4,2,5376]{2,1,0:T(2,128)(2,1)} %reshape.586), calls=%async_computation.2 | async-start | bytes 172032 | tf_op jit(solution)/shard_map/all_to_all | solution.py:141
  235.3 33.0 %copy-start.1 = (bf16[256,256]{1,0:T(8,128)(2,1)S(1)}, bf16[256,256]{1,0:T(8,128)(2,1)}, u32[]{:S(2)}) copy-start(bf16[256,256]{1,0:T(8,128)(2,1)} %param.18) | copy-start | bytes 393220
  257.8 9.1 %all-to-all-start.5 = ((bf16[4,4,2688]{2,1,0:T(4,128)(2,1)}), bf16[4,4,2688]{2,1,0:T(4,128)(2,1)S(1)}, u32[]{:S(2)}, u32[]{:S(2)}) async-start(bf16[4,4,2688]{2,1,0:T(4,128)(2,1)} %get-tuple-element.27), calls=%async_computation.5 | async-start | bytes 172032 | tf_op jit(solution)/shard_map/all_to_all | solution.py:129
where the time goes:
time: 274 us; the launch traced here: 269 us
  other arithmetic  127 us (46%)
  local copies, waits for them, and re-layouts  82.9 us (30%)
  starting transfers between devices  22.2 us (8%)
  matrix products  11.9 us (4%)
  waiting for transfers between devices  11.4 us (4%)
  blocking collectives  10.7 us (4%)
    unnamed x2, other arithmetic  118 us
    unnamed x27, local copies, waits for them, and re-layouts  37.3 us
    all_to_all x1, blocking collectives, per_device(): lax.all_to_all(jnp.take(lax.all_to_all(own_pred, 'dom', split_axis=2, con...  10.7 us
    all_to_all x1, local copies, waits for them, and re-layouts, per_device(): lax.all_to_all(own_pred, 'dom', split_axis=2, concat_axis=0, tiled=True)  10.5 us
    all_to_all x1, local copies, waits for them, and re-layouts, per_device(): lax.all_to_all(state, 'dom', split_axis=2, concat_axis=0, tiled=True)  10.4 us
    reshape x2, local copies, waits for them, and re-layouts, network(): predicted = predicted.reshape(part_count, row_count, flat_width)  9 us
    all_to_all x1, waiting for transfers between devices, network(): lax.all_to_all(columns, 'row', split_axis=1, concat_axis=2, tiled=True)  6 us
    all_to_all x1, starting transfers between devices, per_device(): lax.all_to_all(state, 'dom', split_axis=2, concat_axis=0, tiled=True)  5.73 us
  transfers between devices with their start and end apart: 5, of which 2 were waited for; matrix products, arithmetic and copies ran while one was open for 63% of the time, Pallas kernels for 0%

commit v1 on v0

v1 whole, which is shorter than its diff:
```python
import functools
import math

import jax
import jax.numpy as jnp
import numpy as np
from jax import lax
from jax.experimental import pallas as pl
from jax.experimental.pallas import tpu as pltpu
from jax.sharding import PartitionSpec as P

HEADS = 8
STEPS = 1000
STRIDE = 20
EPS = 1e-06
LANES = 128
VMEM_LIMIT = 48 * 1024 * 1024
F32 = jnp.float32
BF16 = jnp.bfloat16


def dot(lhs, rhs):
    return jnp.dot(lhs, rhs, preferred_element_type=F32)


def dot_nt(lhs, rhs):
    return lax.dot_general(lhs, rhs, (((1,), (1,)), ((), ())), preferred_element_type=F32)


def rms_scale(wide):
    return lax.rsqrt(jnp.mean(wide * wide, axis=-1, keepdims=True) + EPS)


def rms_round(values_in):
    wide = values_in.astype(F32)
    return (wide * rms_scale(wide)).astype(BF16)


def gelu(values_in):
    return jax.nn.gelu(values_in, approximate=True)


def feed_forward(hidden, w_up, w_down):
    gated = gelu(dot(rms_round(hidden), w_up)).astype(BF16)
    return (hidden.astype(F32) + dot(gated, w_down)).astype(BF16)


def lane_ids(shape):
    return lax.broadcasted_iota(jnp.int32, shape, len(shape) - 1)


def shuffle_matrix(width, source_of):
    rows = lax.broadcasted_iota(jnp.int32, (width, width), 0)
    cols = lax.broadcasted_iota(jnp.int32, (width, width), 1)
    return jnp.where(rows == source_of(cols), 1.0, 0.0).astype(BF16)


def tile_halves(half, j):
    tile, lane = j // LANES, j % LANES
    side, rest = lane // (LANES // 2), lane % (LANES // 2)
    return tile * LANES + (rest // half) * 2 * half + side * half + rest % half


def full_halves(width, half, j):
    side, rest = j // (width // 2), j % (width // 2)
    return (rest // half) * 2 * half + side * half + rest % half


def rotary_angles(count, half, lanes):
    rates = np.exp(-math.log(10000.0) * np.arange(half) / half)
    return np.arange(count)[:, None] * rates[np.arange(lanes) % half][None, :]


def unpack_tokens(flat_ref, out_ref, cols, chan):
    count = flat_ref.shape[0]
    lane = lane_ids((count, LANES))
    for col in range(cols):
        tile, shift = divmod(col * chan, LANES)
        piece = flat_ref[:, tile * LANES : (tile + 1) * LANES]
        if shift + chan > LANES:
            after = flat_ref[:, (tile + 1) * LANES : (tile + 2) * LANES]
            piece = jnp.where(lane >= shift, piece, after)
        if shift:
            piece = pltpu.roll(piece, LANES - shift, 1)
        out_ref[pl.ds(col, count, stride=cols), :] = piece


def pack_tokens(tok_ref, out_ref, rows, cols, chan):
    lane = lane_ids((rows, LANES))
    moved = {}

    def shifted(col):
        if col not in moved:
            piece = tok_ref[pl.ds(col, rows, stride=cols), :]
            shift = (col * chan) % LANES
            moved[col] = pltpu.roll(piece, shift, 1) if shift else piece
        return moved[col]

    for tile in range(cols * chan // LANES):
        first, last = tile * LANES // chan, ((tile + 1) * LANES - 1) // chan
        whole = shifted(last)
        for col in range(last - 1, first - 1, -1):
            whole = jnp.where(lane < (col + 1) * chan - tile * LANES, shifted(col), whole)
        out_ref[0, :, tile * LANES : (tile + 1) * LANES] = whole.astype(BF16)


def row_kernel(
    rows, cols, chan,
    state_ref, prev_ref, temb_ref, w_in_ref, w_qkv_ref, w_ao_ref, w_up_ref, w_down_ref, cos_ref, sin_ref,
    out_ref,
    flat_scr, tok_scr,
):
    width = out_ref.shape[-1]
    head = width // HEADS
    half = head // 2
    flat_scr[:rows, :] = state_ref[0].astype(F32)
    flat_scr[rows:, :] = prev_ref[0].astype(F32)
    unpack_tokens(flat_scr, tok_scr, cols, chan)
    count = rows * cols
    w_in = w_in_ref[...].astype(F32)
    blank = jnp.zeros((LANES - chan, width), F32)
    w_state = jnp.concatenate([w_in[:chan], blank], axis=0).astype(BF16)
    w_prev = jnp.concatenate([w_in[chan:], blank], axis=0).astype(BF16)
    hidden = dot(tok_scr[:count].astype(BF16), w_state) + dot(tok_scr[count:].astype(BF16), w_prev)
    hidden = (hidden + temb_ref[...]).astype(BF16)

    pick = shuffle_matrix(width, functools.partial(tile_halves, half))
    w_q = dot(w_qkv_ref[0, :, :width], pick).astype(BF16)
    w_k = dot(w_qkv_ref[0, :, width : 2 * width], pick).astype(BF16)
    w_v = w_qkv_ref[0, :, 2 * width :]
    normed = rms_round(hidden)
    cos, sin = cos_ref[...], sin_ref[...]
    lane = lane_ids((cols, LANES))
    per_tile = LANES // head
    pair = per_tile // 2

    def spin(part):
        scaled = part * rms_scale(part)
        tiles = []
        for t in range(width // LANES):
            piece = scaled[:, t * LANES : (t + 1) * LANES].reshape(rows, cols, LANES)
            swapped = pltpu.roll(piece, LANES // 2, 2)
            tiles.append(piece * cos[None] + swapped * sin[None])
        return tiles

    scale = 1.0 / math.sqrt(head)
    queries = [(x * scale).astype(BF16) for x in spin(dot(normed, w_q))]
    keys = [x.astype(BF16) for x in spin(dot(normed, w_k))]
    values = dot(normed, w_v).astype(BF16).reshape(rows, cols, width)

    mixtures = []
    for row in range(rows):
        outs = []
        for t in range(width // LANES):
            q_tile, k_tile = queries[t][row], keys[t][row]
            v_tile = values[row, :, t * LANES : (t + 1) * LANES]
            results = []
            for side in range(2):
                k_parts, v_parts = [], []
                for n in range(side * pair, (side + 1) * pair):
                    own = (lane % (LANES // 2)) // half == n
                    k_parts.append(jnp.where(own, k_tile, jnp.zeros_like(k_tile)))
                    ones = jnp.where((lane // head) == (n + pair) % per_tile, 1.0, 0.0).astype(BF16)
                    v_parts.append(jnp.where(lane // head == n, v_tile, ones))
                score = dot_nt(q_tile, jnp.concatenate(k_parts, axis=0))
                results.append(dot(jnp.exp(score).astype(BF16), jnp.concatenate(v_parts, axis=0)))
            low = lane < LANES // 2
            top = jnp.where(low, results[0], results[1])
            bottom = pltpu.roll(jnp.where(low, results[1], results[0]), LANES // 2, 1)
            outs.append(top / bottom)
        mixtures.append(jnp.concatenate(outs, axis=-1))
    mixture = jnp.concatenate(mixtures, axis=0).astype(BF16)
    hidden = (hidden.astype(F32) + dot(mixture, w_ao_ref[0])).astype(BF16)
    out_ref[...] = feed_forward(hidden, w_up_ref[0], w_down_ref[0])


def column_kernel(
    blocks, rows, cols, chan,
    me_ref, *refs,
):
    h_refs = refs[:blocks]
    w_qkv_ref, w_ao_ref, w_up_ref, w_down_ref, w_out_ref, cos_ref, sin_ref, out_ref, k_scr, v_scr, tok_scr = refs[blocks:]
    width = h_refs[0].shape[-1]
    head = width // HEADS
    half = head // 2
    wide = width // 2
    pick = shuffle_matrix(width, functools.partial(full_halves, width, half))
    w_q = dot(w_qkv_ref[0, :, :width], pick).astype(BF16)
    w_k = dot(w_qkv_ref[0, :, width : 2 * width], pick).astype(BF16)
    w_v = dot(w_qkv_ref[0, :, 2 * width :], pick).astype(BF16)
    w_ao = lax.dot_general(pick, w_ao_ref[0], (((0,), (0,)), ((), ())), preferred_element_type=F32).astype(BF16)

    def spin(part, block, factor):
        scaled = part * (rms_scale(part) * factor)
        scaled = scaled.reshape(rows, cols, width)
        first = lax.bitwise_xor(me_ref[0], block) * rows
        left, right = [], []
        for row in range(rows):
            cos, sin = cos_ref[pl.ds(first + row, 1), :], sin_ref[pl.ds(first + row, 1), :]
            a, c = scaled[row, :, :wide], scaled[row, :, wide:]
            left.append((a * cos - c * sin).astype(BF16))
            right.append((a * sin + c * cos).astype(BF16))
        return left, right

    own = h_refs[0][...]
    q_left, q_right = spin(dot(rms_round(own), w_q), 0, 1.0 / math.sqrt(head))
    q_left, q_right = jnp.stack(q_left), jnp.stack(q_right)
    for block in range(blocks):
        normed = rms_round(h_refs[block][...])
        left, right = spin(dot(normed, w_k), block, 1.0)
        for row in range(rows):
            k_scr[block * rows + row, :, :wide] = left[row]
            k_scr[block * rows + row, :, wide:] = right[row]
        v_scr[block * rows : (block + 1) * rows] = dot(normed, w_v).astype(BF16).reshape(rows, cols, width)

    ids0 = lax.broadcasted_iota(jnp.int32, (width, width), 0)
    ids1 = lax.broadcasted_iota(jnp.int32, (width, width), 1)
    gather = jnp.where(ids0 // half == ids1 // half, 1.0, 0.0).astype(BF16)
    num_left = jnp.zeros((rows, cols, wide), F32)
    num_right = jnp.zeros((rows, cols, wide), F32)
    den = jnp.zeros((rows, cols, wide), F32)
    for two in range(blocks * rows // 2):
        prods = []
        for key in (2 * two, 2 * two + 1):
            prods.append(q_left * k_scr[key, :, :wide][None] + q_right * k_scr[key, :, wide:][None])
        score = dot(jnp.concatenate(prods, axis=-1).reshape(rows * cols, width), gather)
        weight = jnp.exp(score).reshape(rows, cols, width)
        for side, key in enumerate((2 * two, 2 * two + 1)):
            share = weight[..., side * wide : (side + 1) * wide]
            num_left += share * v_scr[key, :, :wide].astype(F32)[None]
            num_right += share * v_scr[key, :, wide:].astype(F32)[None]
            den += share
    mixture = jnp.concatenate([num_left / den, num_right / den], axis=-1).astype(BF16)
    hidden = (own.astype(F32) + dot(mixture.reshape(rows * cols, width), w_ao)).astype(BF16)
    hidden = feed_forward(hidden, w_up_ref[0], w_down_ref[0])
    tok_scr[:, :chan] = dot(rms_round(hidden), w_out_ref[...])
    pack_tokens(tok_scr, out_ref, rows, cols, chan)


def finish_kernel(count, pick_ref, coef_ref, state_ref, *refs):
    preds = refs[:count]
    new_state_ref, new_pred_ref = refs[count:]
    chosen = preds[0][...]
    for k in range(1, count):
        chosen = jnp.where(pick_ref[1] == k, preds[k][...], chosen)
    new_pred_ref[...] = chosen
    new_state_ref[...] = (coef_ref[0] * chosen.astype(F32) + coef_ref[1] * state_ref[...].astype(F32)).astype(BF16)


def level(moment):
    cosine = jnp.cos((moment / STEPS + 0.008) / 1.008 * math.pi / 2.0)
    return cosine * cosine


def time_vector(timestep, w_time):
    moment = timestep[0].astype(F32)
    half_size = w_time.shape[0] // 2
    rates = jnp.exp(-math.log(10000.0) * jnp.arange(half_size, dtype=F32) / half_size)
    embedded = jnp.concatenate([jnp.sin(moment * rates), jnp.cos(moment * rates)])
    return jnp.dot(embedded, w_time.astype(F32), precision=lax.Precision.HIGHEST)


VMEM_SPEC = pl.BlockSpec(memory_space=pltpu.VMEM)
SMEM_SPEC = pl.BlockSpec(memory_space=pltpu.SMEM)


def exchange(value, axis, size):
    blocks = [value]
    step = size // 2
    order = [0]
    while step:
        pairs = [(i, i ^ step) for i in range(size)]
        blocks = blocks + [lax.ppermute(b, axis, pairs) for b in blocks]
        order = order + [o ^ step for o in order]
        step //= 2
    return [blocks[order.index(b)] for b in range(size)]


def make(mesh):
    n_dom, n_row = mesh.shape["dom"], mesh.shape["row"]

    def per_device(
        state, prev_pred, ancestors, timestep, w_in, w_time, w_qkv, w_attn_out, w_up, w_down, w_out
    ):
        rows, flat = state.shape[1], state.shape[2]
        chan, width = w_out.shape[1], w_out.shape[0]
        cols = flat // chan
        head = width // HEADS
        half = head // 2
        offset_vec = time_vector(timestep, w_time)
        moment = timestep[0].astype(F32)
        now, after = level(moment), level(moment - STRIDE)
        keep = jnp.sqrt(1.0 - after) / jnp.sqrt(1.0 - now)
        coefs = jnp.stack([jnp.sqrt(after) - keep * jnp.sqrt(now), keep])
        all_states = lax.all_gather(state, "dom", tiled=True)
        my_dom = lax.axis_index("dom")
        mine = ancestors[my_dom]
        params = pltpu.CompilerParams(vmem_limit_bytes=VMEM_LIMIT)

        along = rotary_angles(cols, half, LANES)
        sign = np.where(np.arange(LANES) < LANES // 2, -1.0, 1.0)
        block_of = lambda i: lambda *_: (i, 0, 0)
        per_block = lambda arr, i: pl.BlockSpec((1,) + arr.shape[1:], block_of(i))
        whole = lambda arr: pl.BlockSpec(arr.shape, lambda *_: (0,) * arr.ndim)
        tables = [jnp.asarray(np.cos(along), F32), jnp.asarray(np.sin(along) * sign, F32)]
        temb = offset_vec[None, :]
        hidden = pl.pallas_call(
            functools.partial(row_kernel, rows, cols, chan),
            grid=(1,),
            out_shape=jax.ShapeDtypeStruct((rows * cols, width), BF16),
            in_specs=[
                whole(state), whole(prev_pred), whole(temb), whole(w_in),
                per_block(w_qkv, 0), per_block(w_attn_out, 0), per_block(w_up, 0), per_block(w_down, 0),
                whole(tables[0]), whole(tables[1]),
            ],
            out_specs=pl.BlockSpec((rows * cols, width), lambda *_: (0, 0)),
            scratch_shapes=[
                pltpu.VMEM((2 * rows, flat), F32),
                pltpu.VMEM((2 * rows * cols, LANES), F32),
            ],
            compiler_params=params,
            name="row_block",
        )(state, prev_pred, temb, w_in, w_qkv, w_attn_out, w_up, w_down, *tables)

        blocks = exchange(hidden, "row", n_row)
        down = rotary_angles(n_row * rows, half, width // 2)
        tables = [jnp.asarray(np.cos(down), F32), jnp.asarray(np.sin(down), F32)]
        me = lax.axis_index("row").astype(jnp.int32)[None]
        own_pred = pl.pallas_call(
            functools.partial(column_kernel, n_row, rows, cols, chan),
            grid=(1,),
            out_shape=jax.ShapeDtypeStruct((1, rows, flat), BF16),
            in_specs=[SMEM_SPEC]
            + [whole(hidden)] * n_row
            + [
                per_block(w_qkv, 1), per_block(w_attn_out, 1), per_block(w_up, 1), per_block(w_down, 1),
                whole(w_out), whole(tables[0]), whole(tables[1]),
            ],
            out_specs=pl.BlockSpec((1, rows, flat), lambda *_: (0, 0, 0)),
            scratch_shapes=[
                pltpu.VMEM((n_row * rows, cols, width), BF16),
                pltpu.VMEM((n_row * rows, cols, width), BF16),
                pltpu.VMEM((rows * cols, LANES), F32),
            ],
            compiler_params=params,
            name="column_block",
        )(me, *blocks, w_qkv, w_attn_out, w_up, w_down, w_out, *tables)

        if n_dom & (n_dom - 1) == 0 and n_dom <= 8:
            preds = [own_pred] + [
                lax.ppermute(own_pred, "dom", [(i, i ^ k) for i in range(n_dom)]) for k in range(1, n_dom)
            ]
            choice = jnp.bitwise_xor(mine, my_dom)
        else:
            preds = [lax.dynamic_index_in_dim(lax.all_gather(own_pred, "dom"), mine, 0, keepdims=False)]
            choice = jnp.zeros_like(mine)
        shape = jax.ShapeDtypeStruct(state.shape, BF16)
        picks = jnp.stack([mine, choice]).astype(jnp.int32)
        return pl.pallas_call(
            functools.partial(finish_kernel, len(preds)),
            out_shape=(shape, shape),
            grid_spec=pltpu.PrefetchScalarGridSpec(
                num_scalar_prefetch=1,
                grid=(1,),
                in_specs=[SMEM_SPEC, pl.BlockSpec(state.shape, lambda _, pick: (pick[0], 0, 0))]
                + [pl.BlockSpec(state.shape, lambda *_: (0, 0, 0))] * len(preds),
                out_specs=[pl.BlockSpec(state.shape, lambda *_: (0, 0, 0))] * 2,
            ),
            compiler_params=params,
            name="finish",
        )(picks, coefs, all_states, *preds)

    return per_device


def solution(mesh):
    spread = P(("group", "dom"), "row", None)
    return jax.shard_map(
        make(mesh),
        mesh=mesh,
        in_specs=(spread, spread, P("group"), P("group")) + (P(),) * 7,
        out_specs=(spread, spread),
        check_vma=False,
    )
```

time: 274 us -> 60.1 us (0.22); the launches traced: 269 us -> 59.6 us
  other arithmetic: 127 us -> 0.85 us
  local copies, waits for them, and re-layouts: 82.9 us -> 10.1 us
  starting transfers between devices: 22.2 us -> 7.77 us
  Pallas kernels: 0 us -> 11.8 us
  matrix products: 11.9 us -> 0.13 us
  blocking collectives: 10.7 us -> 15.4 us
    unnamed x2 -> x0, other arithmetic: 118 us -> none
    unnamed x27 -> x37, local copies, waits for them, and re-layouts: 37.3 us -> 9.56 us
    all_to_all x5 -> x0, starting transfers between devices: 22.2 us -> none  [the longest x1 5.73 us: per_device(): lax.all_to_all(state, 'dom', split_axis=2, concat_axis=0, tiled=True)]
    all_to_all x2 -> x0, local copies, waits for them, and re-layouts: 20.9 us -> none  [the longest x1 10.5 us: per_device(): lax.all_to_all(own_pred, 'dom', split_axis=2, concat_axis=0, tiled=True)]
    reshape x9 -> x0, local copies, waits for them, and re-layouts: 16.5 us -> none  [the longest x2 9 us: network(): predicted = predicted.reshape(part_count, row_count, flat_width)]
    all_gather x0 -> x1, blocking collectives: none -> 15.4 us  [per_device(): all_states = lax.all_gather(state, 'dom', tiled=True)]
    pallas_call x0 -> x3, Pallas kernels: none -> 11.8 us  [the longest x1 5.71 us: per_device(): pl.pallas_call(functools.partial(column_kernel, n_row, rows, cols, chan),...]
    dot_general x13 -> x1, matrix products: 11.9 us -> 0.13 us  [time_vector(): jnp.dot(embedded, w_time.astype(F32), precision=lax.Precision.HIGHEST)]
  transfers between devices with their start and end apart: 5 -> 6, of which waited for: 2 -> 3; matrix products, arithmetic and copies ran while one was open for 63% -> 5% of each run, Pallas kernels for 0% -> 0%
where the time goes in v1:
time: 60.1 us; the launch traced here: 59.6 us
  blocking collectives  15.4 us (26%)
  Pallas kernels  11.8 us (20%)
  waiting for transfers between devices  11.1 us (18%)
  local copies, waits for them, and re-layouts  10.1 us (17%)
  starting transfers between devices  7.77 us (13%)
  between operations  2.46 us (4%)
  other arithmetic  0.85 us (1%)
    all_gather x1, blocking collectives, per_device(): all_states = lax.all_gather(state, 'dom', tiled=True)  15.4 us
    unnamed x37, local copies, waits for them, and re-layouts  9.56 us
    ppermute x3, waiting for transfers between devices, exchange(): blocks = blocks + [lax.ppermute(b, axis, pairs) for b in blocks]  6.42 us
    pallas_call x1, Pallas kernels, per_device(): pl.pallas_call(functools.partial(column_kernel, n_row, rows, cols, chan),...  5.71 us
    ppermute x3, starting transfers between devices, per_device(): lax.ppermute(own_pred, 'dom', [(i, i ^ k) for i in range(n_dom)])  4.76 us
    ppermute x3, waiting for transfers between devices, per_device(): lax.ppermute(own_pred, 'dom', [(i, i ^ k) for i in range(n_dom)])  4.69 us
    pallas_call x1, Pallas kernels, per_device(): pl.pallas_call(functools.partial(row_kernel, rows, cols, chan), grid=(1,)...  4.29 us
    ppermute x3, starting transfers between devices, exchange(): blocks = blocks + [lax.ppermute(b, axis, pairs) for b in blocks]  3.01 us
  transfers between devices with their start and end apart: 6, of which 3 were waited for; matrix products, arithmetic and copies ran while one was open for 5% of the time, Pallas kernels for 0%

profile of v1, /device:TPU:0, one launch (start us, length us, event | category | flops | bytes accessed | tf_op | source)
XLA Modules:
  0.0 59.6 jit_solution(3042716972046322385)
XLA Ops:
  1.4 0.1 copy-done
  1.5 0.1 fusion.2.temb_ref
  1.7 1.2 %copy-done.1 = bf16[2,256,1024]{2,1,0:T(8,128)(2,1)S(1)} copy-done((bf16[2,256,1024]{2,1,0:T(8,128)(2,1)S(1)}, bf16[2,256,1024]{2,1,0:T(8,128)(2,1)}, u32[]{:S(2)}) %copy-start.1) | copy-done | bytes 1048600
  3.0 1.2 %copy-done.3 = bf16[2,1024,256]{2,1,0:T(8,128)(2,1)S(1)} copy-done((bf16[2,1024,256]{2,1,0:T(8,128)(2,1)S(1)}, bf16[2,1024,256]{2,1,0:T(8,128)(2,1)}, u32[]{:S(2)}) %copy-start.3) | copy-done | bytes 1048600
  4.2 1.1 %copy-done.5 = bf16[2,256,768]{2,1,0:T(8,128)(2,1)S(1)} copy-done((bf16[2,256,768]{2,1,0:T(8,128)(2,1)S(1)}, bf16[2,256,768]{2,1,0:T(8,128)(2,1)}, u32[]{:S(2)}) %copy-start.5) | copy-done | bytes 786456
  5.3 0.9 %copy-done.7 = bf16[2,256,256]{2,1,0:T(8,128)(2,1)S(1)} copy-done((bf16[2,256,256]{2,1,0:T(8,128)(2,1)S(1)}, bf16[2,256,256]{2,1,0:T(8,128)(2,1)}, u32[]{:S(2)}) %copy-start.7) | copy-done | bytes 262168
  6.3 0.9 %copy-done.11 = bf16[1,4,10752]{2,1,0:T(4,128)(2,1)S(1)} copy-done((bf16[1,4,10752]{2,1,0:T(4,128)(2,1)S(1)}, bf16[1,4,10752]{2,1,0:T(4,128)(2,1)}, u32[]{:S(2)}) %copy-start.11) | copy-done | bytes 86040
  7.2 0.9 %copy-done.12 = bf16[168,256]{1,0:T(8,128)(2,1)S(1)} copy-done((bf16[168,256]{1,0:T(8,128)(2,1)S(1)}, bf16[168,256]{1,0:T(8,128)(2,1)}, u32[]{:S(2)}) %copy-start.12) | copy-done | bytes 86040
  8.0 0.8 %copy-done.14 = f32[128,128]{1,0:T(8,128)S(1)} copy-done((f32[128,128]{1,0:T(8,128)S(1)}, f32[128,128]{1,0:T(8,128)}, u32[]{:S(2)}) %copy-start.14) | copy-done | bytes 65560
  8.9 4.3 %row_block.1.refs_0_ = bf16[512,256]{1,0:T(8,128)(2,1)S(1)} custom-call(bf16[1,4,10752]{2,1,0:T(4,128)(2,1)S(1)} %copy-done.9, bf16[1,4,10752]{2,1,0:T(4,128)(2,1)S(1)} %copy-done.11, f32[1,256]{1,0:T(1,128)S(1)} %fusion.2.temb_ref, bf16[168,256]{1,0:T(8,128)(2,1)S(1)} %copy-done.12, bf16[2,256,768]{2,1,0:T(8,128)(2,1)S(1)} %copy-done.5, ...), custom_call_target="tpu_custom_call" | custom-call | tf_op jit(solution)/shard_map/row_block/pallas_call | solution.py:307
  13.2 3.0 %collective-permute-start.1 = (bf16[512,256]{1,0:T(8,128)(2,1)S(1)}, bf16[512,256]{1,0:T(8,128)(2,1)}, u32[]{:S(2)}, u32[]{:S(2)}) collective-permute-start(bf16[512,256]{1,0:T(8,128)(2,1)S(1)} %row_block.1.refs_0_), channel_id=1, source_target_pairs={{0,2},{1,3},{2,0},{3,1},{4,6},{5,7},{6,4},{7,5},{8,10},{9,11},{10,... | collective-permute-start | bytes 786440 | tf_op jit(solution)/shard_map/ppermute | solution.py:273
  16.2 6.4 %collective-permute-done.1.refs_2_ = bf16[512,256]{1,0:T(8,128)(2,1)} collective-permute-done((bf16[512,256]{1,0:T(8,128)(2,1)S(1)}, bf16[512,256]{1,0:T(8,128)(2,1)}, u32[]{:S(2)}, u32[]{:S(2)}) %collective-permute-start.1) | collective-permute-done | bytes 262176 | tf_op jit(solution)/shard_map/ppermute | solution.py:273
  23.0 0.6 %copy-done.17 = s32[4]{0:T(128)S(1)} copy-done((s32[4]{0:T(128)S(1)}, s32[4]{0:T(128)}, u32[]{:S(2)}) %copy-start.17) | copy-done | bytes 40
  23.6 0.6 dynamic_slice.3
  24.8 1.6 %copy.18.refs_8_ = bf16[256,84]{1,0:T(8,128)(2,1)} copy(bf16[256,84]{0,1:T(8,128)(2,1)} %param.25) | data formatting | bytes 86016 | tf_op args[10]
  26.4 0.7 %pad_add_fusion.pick_ref = s32[2]{0:T(128)S(1)} fusion(s32[1]{0:T(128)} %bitcast.1, s32[1]{0:T(128)} %dynamic_slice.3), kind=kLoop, calls=%fused_computation.1 | loop fusion | flops 2 | bytes 16 | tf_op jit(solution)/shard_map/stack | solution.py:358
  27.1 15.4 %all_gather.3.state_ref = bf16[4,4,10752]{2,1,0:T(4,128)(2,1)S(1)} all-gather(bf16[1,4,10752]{2,1,0:T(4,128)(2,1)} %state_ref.1), channel_id=1, replica_groups=mesh['group'=2,'dom'=4,'row'=4] {'dom'}, dimensions={0}, use_global_device_ids=true | all-gather | bytes 430080 | tf_op jit(solution)/shard_map/all_gather | solution.py:295
  42.6 5.7 %column_block.1.refs_0_ = bf16[1,4,10752]{2,1,0:T(4,128)(2,1)S(1)} custom-call(s32[1]{0:T(128)} %bitcast.5.me_ref, bf16[512,256]{1,0:T(8,128)(2,1)S(1)} %row_block.1.refs_0_, bf16[512,256]{1,0:T(8,128)(2,1)} %collective-permute-done.refs_1_, bf16[512,256]{1,0:T(8,128)(2,1)} %collective-permute-done.1.refs_2_, ...), custom_call_target="tpu_custom_call" | custom-call | tf_op jit(solution)/shard_map/column_block/pallas_call | solution.py:329
  48.3 4.1 %collective-permute-start.5 = (bf16[1,4,10752]{2,1,0:T(4,128)(2,1)S(1)}, bf16[1,4,10752]{2,1,0:T(4,128)(2,1)S(1)}, u32[]{:S(2)}, u32[]{:S(2)}) collective-permute-start(bf16[1,4,10752]{2,1,0:T(4,128)(2,1)S(1)} %column_block.1.refs_0_), channel_id=1, source_target_pairs={{0,12},{4,8},{8,4},{12,0},{1,13},{5,9},{9,5},{13,1},{2,14},{6,10},... | collective-permute-start | bytes 258056 | tf_op jit(solution)/shard_map/ppermute | solution.py:351
  52.4 0.6 %collective-permute-start.3 = (bf16[1,4,10752]{2,1,0:T(4,128)(2,1)S(1)}, bf16[1,4,10752]{2,1,0:T(4,128)(2,1)S(1)}, u32[]{:S(2)}, u32[]{:S(2)}) collective-permute-start(bf16[1,4,10752]{2,1,0:T(4,128)(2,1)S(1)} %column_block.1.refs_0_), channel_id=1, source_target_pairs={{0,4},{4,0},{8,12},{12,8},{1,5},{5,1},{9,13},{13,9},{2,6},{6,2},{1... | collective-permute-start | bytes 258056 | tf_op jit(solution)/shard_map/ppermute | solution.py:351
  53.1 0.1 pad_maximum_fusion.1.coef_ref
  53.1 2.6 %collective-permute-done.5.refs_3_ = bf16[1,4,10752]{2,1,0:T(4,128)(2,1)S(1)} collective-permute-done((bf16[1,4,10752]{2,1,0:T(4,128)(2,1)S(1)}, bf16[1,4,10752]{2,1,0:T(4,128)(2,1)S(1)}, u32[]{:S(2)}, u32[]{:S(2)}) %collective-permute-start.5) | collective-permute-done | bytes 86048 | tf_op jit(solution)/shard_map/ppermute | solution.py:351
  55.7 2.1 %collective-permute-done.4.refs_2_ = bf16[1,4,10752]{2,1,0:T(4,128)(2,1)S(1)} collective-permute-done((bf16[1,4,10752]{2,1,0:T(4,128)(2,1)S(1)}, bf16[1,4,10752]{2,1,0:T(4,128)(2,1)S(1)}, u32[]{:S(2)}, u32[]{:S(2)}) %collective-permute-start.4) | collective-permute-done | bytes 86048 | tf_op jit(solution)/shard_map/ppermute | solution.py:351
  57.8 1.8 %finish.1 = (bf16[1,4,10752]{2,1,0:T(4,128)(2,1)}, bf16[1,4,10752]{2,1,0:T(4,128)(2,1)}) custom-call(s32[2]{0:T(128)S(1)} %pad_add_fusion.pick_ref, f32[2]{0:T(128)S(1)} %pad_maximum_fusion.1.coef_ref, bf16[4,4,10752]{2,1,0:T(4,128)(2,1)S(1)} %all_gather.3.state_ref, bf16[1,4,10752]{2,1,0:T(4,128)(2,1)S(1)} %column_block.1.refs_0_, ...), custom_call_target="tpu_custom_call" | custom-call | tf_op jit(solution)/shard_map/finish/pallas_call | solution.py:359
  (35 shorter events, 0.2 us)
Async XLA Ops:
  0.6 0.9 %copy-start = (bf16[256,256]{1,0:T(8,128)(2,1)S(1)}, bf16[256,256]{1,0:T(8,128)(2,1)}, u32[]{:S(2)}) copy-start(bf16[256,256]{1,0:T(8,128)(2,1)} %param.20) | copy-start | bytes 393220
  0.6 1.0 %copy-start.13 = (f32[128,128]{1,0:T(8,128)S(1)}, f32[128,128]{1,0:T(8,128)}, u32[]{:S(2)}) copy-start(f32[128,128]{1,0:T(8,128)} %constant.48.clone.sin_ref) | copy-start | bytes 196612
  0.7 1.0 %copy-start.9 = (bf16[1,4,10752]{2,1,0:T(4,128)(2,1)S(1)}, bf16[1,4,10752]{2,1,0:T(4,128)(2,1)}, u32[]{:S(2)}) copy-start(bf16[1,4,10752]{2,1,0:T(4,128)(2,1)} %state_ref.1) | copy-start | bytes 258052
  1.7 1.3 %copy-start.1 = (bf16[2,256,1024]{2,1,0:T(8,128)(2,1)S(1)}, bf16[2,256,1024]{2,1,0:T(8,128)(2,1)}, u32[]{:S(2)}) copy-start(bf16[2,256,1024]{2,1,0:T(8,128)(2,1)} %refs_6_.1) | copy-start | bytes 3145732
  3.0 1.2 %copy-start.3 = (bf16[2,1024,256]{2,1,0:T(8,128)(2,1)S(1)}, bf16[2,1024,256]{2,1,0:T(8,128)(2,1)}, u32[]{:S(2)}) copy-start(bf16[2,1024,256]{2,1,0:T(8,128)(2,1)} %refs_7_.1) | copy-start | bytes 3145732
  4.2 1.1 %copy-start.5 = (bf16[2,256,768]{2,1,0:T(8,128)(2,1)S(1)}, bf16[2,256,768]{2,1,0:T(8,128)(2,1)}, u32[]{:S(2)}) copy-start(bf16[2,256,768]{2,1,0:T(8,128)(2,1)} %refs_4_.1) | copy-start | bytes 2359300
  5.3 0.9 %copy-start.7 = (bf16[2,256,256]{2,1,0:T(8,128)(2,1)S(1)}, bf16[2,256,256]{2,1,0:T(8,128)(2,1)}, u32[]{:S(2)}) copy-start(bf16[2,256,256]{2,1,0:T(8,128)(2,1)} %refs_5_.1) | copy-start | bytes 786436
  6.3 0.9 %copy-start.11 = (bf16[1,4,10752]{2,1,0:T(4,128)(2,1)S(1)}, bf16[1,4,10752]{2,1,0:T(4,128)(2,1)}, u32[]{:S(2)}) copy-start(bf16[1,4,10752]{2,1,0:T(4,128)(2,1)} %prev_ref.1) | copy-start | bytes 258052
  7.2 0.9 %copy-start.12 = (bf16[168,256]{1,0:T(8,128)(2,1)S(1)}, bf16[168,256]{1,0:T(8,128)(2,1)}, u32[]{:S(2)}) copy-start(bf16[168,256]{1,0:T(8,128)(2,1)} %w_in_ref.1) | copy-start | bytes 258052
  8.0 0.8 %copy-start.14 = (f32[128,128]{1,0:T(8,128)S(1)}, f32[128,128]{1,0:T(8,128)}, u32[]{:S(2)}) copy-start(f32[128,128]{1,0:T(8,128)} %constant.47.clone.cos_ref) | copy-start | bytes 196612
  8.9 33.6 %copy-start.2 = (bf16[2,256,1024]{2,1,0:T(8,128)(2,1)S(1)}, bf16[2,256,1024]{2,1,0:T(8,128)(2,1)}, u32[]{:S(2)}) copy-start(bf16[2,256,1024]{2,1,0:T(8,128)(2,1)} %refs_6_.1) | copy-start | bytes 3145732
  8.9 33.6 %copy-start.4 = (bf16[2,1024,256]{2,1,0:T(8,128)(2,1)S(1)}, bf16[2,1024,256]{2,1,0:T(8,128)(2,1)}, u32[]{:S(2)}) copy-start(bf16[2,1024,256]{2,1,0:T(8,128)(2,1)} %refs_7_.1) | copy-start | bytes 3145732
  8.9 33.6 %copy-start.6 = (bf16[2,256,768]{2,1,0:T(8,128)(2,1)S(1)}, bf16[2,256,768]{2,1,0:T(8,128)(2,1)}, u32[]{:S(2)}) copy-start(bf16[2,256,768]{2,1,0:T(8,128)(2,1)} %refs_4_.1) | copy-start | bytes 2359300
  13.2 9.4 %collective-permute-start.1 = (bf16[512,256]{1,0:T(8,128)(2,1)S(1)}, bf16[512,256]{1,0:T(8,128)(2,1)}, u32[]{:S(2)}, u32[]{:S(2)}) collective-permute-start(bf16[512,256]{1,0:T(8,128)(2,1)S(1)} %row_block.1.refs_0_), channel_id=1, source_target_pairs={{0,2},{1,3},{2,0},{3,1},{4,6},{5,7},{6,4},{7,5},{8,10},{9,11},{10,... | collective-permute-start | bytes 786440 | tf_op jit(solution)/shard_map/ppermute | solution.py:273
  16.2 26.3 %collective-permute-start = (bf16[512,256]{1,0:T(8,128)(2,1)S(1)}, bf16[512,256]{1,0:T(8,128)(2,1)}, u32[]{:S(2)}, u32[]{:S(2)}) collective-permute-start(bf16[512,256]{1,0:T(8,128)(2,1)S(1)} %row_block.1.refs_0_), channel_id=1, source_target_pairs={{0,1},{1,0},{2,3},{3,2},{4,5},{5,4},{6,7},{7,6},{8,9},{9,8},{10,11... | collective-permute-start | bytes 786440 | tf_op jit(solution)/shard_map/ppermute | solution.py:273
  22.6 19.9 %collective-permute-start.2 = (bf16[512,256]{1,0:T(8,128)(2,1)}, bf16[512,256]{1,0:T(8,128)(2,1)}, u32[]{:S(2)}, u32[]{:S(2)}) collective-permute-start(bf16[512,256]{1,0:T(8,128)(2,1)} %collective-permute-done.1.refs_2_), channel_id=1, source_target_pairs={{0,1},{1,0},{2,3},{3,2},{4,5},{5,4},{6,7},{7,6},{8,9},{9,8},{10,11... | collective-permute-start | bytes 786440 | tf_op jit(solution)/shard_map/ppermute | solution.py:273
  22.9 0.7 %copy-start.17 = (s32[4]{0:T(128)S(1)}, s32[4]{0:T(128)}, u32[]{:S(2)}) copy-start(s32[4]{0:T(128)} %param.17) | copy-start | bytes 52
  24.8 17.7 %copy-start.8 = (bf16[2,256,256]{2,1,0:T(8,128)(2,1)S(1)}, bf16[2,256,256]{2,1,0:T(8,128)(2,1)}, u32[]{:S(2)}) copy-start(bf16[2,256,256]{2,1,0:T(8,128)(2,1)} %refs_5_.1) | copy-start | bytes 786436
  27.1 15.4 %copy-start.10 = (bf16[256,84]{1,0:T(8,128)(2,1)S(1)}, bf16[256,84]{1,0:T(8,128)(2,1)}, u32[]{:S(2)}) copy-start(bf16[256,84]{1,0:T(8,128)(2,1)} %copy.18.refs_8_) | copy-start | bytes 129028
  27.1 15.4 %copy-start.15 = (f32[16,128]{1,0:T(8,128)S(1)}, f32[16,128]{1,0:T(8,128)}, u32[]{:S(2)}) copy-start(f32[16,128]{1,0:T(8,128)} %constant.50.clone.refs_10_) | copy-start | bytes 24580
  27.1 15.4 %copy-start.16 = (f32[16,128]{1,0:T(8,128)S(1)}, f32[16,128]{1,0:T(8,128)}, u32[]{:S(2)}) copy-start(f32[16,128]{1,0:T(8,128)} %constant.49.clone.refs_9_) | copy-start | bytes 24580
  48.3 7.4 %collective-permute-start.5 = (bf16[1,4,10752]{2,1,0:T(4,128)(2,1)S(1)}, bf16[1,4,10752]{2,1,0:T(4,128)(2,1)S(1)}, u32[]{:S(2)}, u32[]{:S(2)}) collective-permute-start(bf16[1,4,10752]{2,1,0:T(4,128)(2,1)S(1)} %column_block.1.refs_0_), channel_id=1, source_target_pairs={{0,12},{4,8},{8,4},{12,0},{1,13},{5,9},{9,5},{13,1},{2,14},{6,10},... | collective-permute-start | bytes 258056 | tf_op jit(solution)/shard_map/ppermute | solution.py:351
  52.4 5.4 %collective-permute-start.4 = (bf16[1,4,10752]{2,1,0:T(4,128)(2,1)S(1)}, bf16[1,4,10752]{2,1,0:T(4,128)(2,1)S(1)}, u32[]{:S(2)}, u32[]{:S(2)}) collective-permute-start(bf16[1,4,10752]{2,1,0:T(4,128)(2,1)S(1)} %column_block.1.refs_0_), channel_id=1, source_target_pairs={{0,8},{4,12},{8,0},{12,4},{1,9},{5,13},{9,1},{13,5},{2,10},{6,14},... | collective-permute-start | bytes 258056 | tf_op jit(solution)/shard_map/ppermute | solution.py:351
  52.4 5.4 %collective-permute-start.3 = (bf16[1,4,10752]{2,1,0:T(4,128)(2,1)S(1)}, bf16[1,4,10752]{2,1,0:T(4,128)(2,1)S(1)}, u32[]{:S(2)}, u32[]{:S(2)}) collective-permute-start(bf16[1,4,10752]{2,1,0:T(4,128)(2,1)S(1)} %column_block.1.refs_0_), channel_id=1, source_target_pairs={{0,4},{4,0},{8,12},{12,8},{1,5},{5,1},{9,13},{13,9},{2,6},{6,2},{1... | collective-permute-start | bytes 258056 | tf_op jit(solution)/shard_map/ppermute | solution.py:351

commit v2 on v1

v2 whole, which is shorter than its diff:
```python
import functools
import math

import jax
import jax.numpy as jnp
import numpy as np
from jax import lax
from jax.experimental import pallas as pl
from jax.experimental.pallas import tpu as pltpu
from jax.sharding import PartitionSpec as P

HEADS = 8
STEPS = 1000
STRIDE = 20
EPS = 1e-06
LANES = 128
VMEM_LIMIT = 32 * 1024 * 1024
ROW_VMEM_LIMIT = 62 * 1024 * 1024
WORK_UNIT = 1 << 30
F32 = jnp.float32
BF16 = jnp.bfloat16


def dot(lhs, rhs):
    return jnp.dot(lhs, rhs, preferred_element_type=F32)


def dot_nt(lhs, rhs):
    return lax.dot_general(lhs, rhs, (((1,), (1,)), ((), ())), preferred_element_type=F32)


def rms_scale(wide):
    return lax.rsqrt(jnp.mean(wide * wide, axis=-1, keepdims=True) + EPS)


def rms_round(values_in):
    wide = values_in.astype(F32)
    return (wide * rms_scale(wide)).astype(BF16)


def gelu(values_in):
    return jax.nn.gelu(values_in, approximate=True)


def feed_forward(hidden, w_up, w_down):
    gated = gelu(dot(rms_round(hidden), w_up)).astype(BF16)
    return (hidden.astype(F32) + dot(gated, w_down)).astype(BF16)


def lane_ids(shape):
    return lax.broadcasted_iota(jnp.int32, shape, len(shape) - 1)


def shuffle_matrix(width, source_of):
    rows = lax.broadcasted_iota(jnp.int32, (width, width), 0)
    cols = lax.broadcasted_iota(jnp.int32, (width, width), 1)
    return jnp.where(rows == source_of(cols), 1.0, 0.0).astype(BF16)


def tile_halves(half, j):
    tile, lane = j // LANES, j % LANES
    side, rest = lane // (LANES // 2), lane % (LANES // 2)
    return tile * LANES + (rest // half) * 2 * half + side * half + rest % half


def full_halves(width, half, j):
    side, rest = j // (width // 2), j % (width // 2)
    return (rest // half) * 2 * half + side * half + rest % half


def rotary_angles(count, half, lanes):
    rates = np.exp(-math.log(10000.0) * np.arange(half) / half)
    return np.arange(count)[:, None] * rates[np.arange(lanes) % half][None, :]


def unpack_tokens(flat_ref, out_ref, cols, chan):
    count = flat_ref.shape[0]
    lane = lane_ids((count, LANES))
    for col in range(cols):
        tile, shift = divmod(col * chan, LANES)
        piece = flat_ref[:, tile * LANES : (tile + 1) * LANES]
        if shift + chan > LANES:
            after = flat_ref[:, (tile + 1) * LANES : (tile + 2) * LANES]
            piece = jnp.where(lane >= shift, piece, after)
        if shift:
            piece = pltpu.roll(piece, LANES - shift, 1)
        out_ref[pl.ds(col, count, stride=cols), :] = piece


def pack_tokens(tok_ref, out_ref, rows, cols, chan):
    lane = lane_ids((rows, LANES))
    moved = {}

    def shifted(col):
        if col not in moved:
            piece = tok_ref[pl.ds(col, rows, stride=cols), :]
            shift = (col * chan) % LANES
            moved[col] = pltpu.roll(piece, shift, 1) if shift else piece
        return moved[col]

    for tile in range(cols * chan // LANES):
        first, last = tile * LANES // chan, ((tile + 1) * LANES - 1) // chan
        whole = shifted(last)
        for col in range(last - 1, first - 1, -1):
            whole = jnp.where(lane < (col + 1) * chan - tile * LANES, shifted(col), whole)
        out_ref[0, :, tile * LANES : (tile + 1) * LANES] = whole.astype(BF16)


def time_vector(moment, w_time):
    half = w_time.shape[0] // 2
    rates = jnp.exp(lane_ids((1, half)).astype(F32) * (-math.log(10000.0) / half))
    angles = moment * rates
    embedded = jnp.concatenate([jnp.sin(angles), jnp.cos(angles)], axis=-1)
    first = embedded.astype(BF16)
    rest = embedded - first.astype(F32)
    second = rest.astype(BF16)
    third = (rest - second.astype(F32)).astype(BF16)
    return dot(first, w_time) + dot(second, w_time) + dot(third, w_time)


def row_kernel(
    rows, cols, chan,
    time_ref, state_ref, prev_ref, w_time_ref, w_in_ref, w_qkv_ref, w_ao_ref, w_up_ref, w_down_ref, cos_ref, sin_ref,
    out_ref,
    time_scr, state_scr, prev_scr, w_time_scr, w_in_scr, w_qkv_scr, w_ao_scr, w_up_scr, w_down_scr, cos_scr, sin_scr,
    flat_scr, tok_scr, sems,
):
    sources = (
        time_ref, state_ref, prev_ref, w_time_ref, w_in_ref, w_qkv_ref.at[0], cos_ref, sin_ref,
        w_ao_ref.at[0], w_up_ref.at[0], w_down_ref.at[0],
    )
    targets = (
        time_scr, state_scr, prev_scr, w_time_scr, w_in_scr, w_qkv_scr, cos_scr, sin_scr,
        w_ao_scr, w_up_scr, w_down_scr,
    )
    copies = [pltpu.make_async_copy(s, t, sems.at[i]) for i, (s, t) in enumerate(zip(sources, targets))]
    for copy in copies:
        copy.start()
    width = out_ref.shape[-1]
    head = width // HEADS
    half = head // 2
    copies[0].wait()
    copies[1].wait()
    flat_scr[:rows, :] = state_scr[0].astype(F32)
    copies[2].wait()
    flat_scr[rows:, :] = prev_scr[0].astype(F32)
    unpack_tokens(flat_scr, tok_scr, cols, chan)
    count = rows * cols
    copies[3].wait()
    offset_vec = time_vector(time_scr[0].astype(F32), w_time_scr[...])
    copies[4].wait()
    w_in = w_in_scr[...].astype(F32)
    blank = jnp.zeros((LANES - chan, width), F32)
    w_state = jnp.concatenate([w_in[:chan], blank], axis=0).astype(BF16)
    w_prev = jnp.concatenate([w_in[chan:], blank], axis=0).astype(BF16)
    hidden = dot(tok_scr[:count].astype(BF16), w_state) + dot(tok_scr[count:].astype(BF16), w_prev)
    hidden = (hidden + offset_vec).astype(BF16)

    copies[5].wait()
    copies[6].wait()
    copies[7].wait()
    pick = shuffle_matrix(width, functools.partial(tile_halves, half))
    w_q = dot(w_qkv_scr[:, :width], pick).astype(BF16)
    w_k = dot(w_qkv_scr[:, width : 2 * width], pick).astype(BF16)
    w_v = w_qkv_scr[:, 2 * width :]
    normed = rms_round(hidden)
    cos, sin = cos_scr[...], sin_scr[...]
    lane = lane_ids((cols, LANES))
    per_tile = LANES // head
    pair = per_tile // 2

    def spin(part):
        scaled = part * rms_scale(part)
        tiles = []
        for t in range(width // LANES):
            piece = scaled[:, t * LANES : (t + 1) * LANES].reshape(rows, cols, LANES)
            swapped = pltpu.roll(piece, LANES // 2, 2)
            tiles.append(piece * cos[None] + swapped * sin[None])
        return tiles

    scale = 1.0 / math.sqrt(head)
    queries = [(x * scale).astype(BF16) for x in spin(dot(normed, w_q))]
    keys = [x.astype(BF16) for x in spin(dot(normed, w_k))]
    values = dot(normed, w_v).astype(BF16).reshape(rows, cols, width)

    mixtures = []
    for row in range(rows):
        outs = []
        for t in range(width // LANES):
            q_tile, k_tile = queries[t][row], keys[t][row]
            v_tile = values[row, :, t * LANES : (t + 1) * LANES]
            results = []
            for side in range(2):
                k_parts, v_parts = [], []
                for n in range(side * pair, (side + 1) * pair):
                    own = (lane % (LANES // 2)) // half == n
                    k_parts.append(jnp.where(own, k_tile, jnp.zeros_like(k_tile)))
                    ones = jnp.where((lane // head) == (n + pair) % per_tile, 1.0, 0.0).astype(BF16)
                    v_parts.append(jnp.where(lane // head == n, v_tile, ones))
                score = dot_nt(q_tile, jnp.concatenate(k_parts, axis=0))
                results.append(dot(jnp.exp(score).astype(BF16), jnp.concatenate(v_parts, axis=0)))
            low = lane < LANES // 2
            top = jnp.where(low, results[0], results[1])
            bottom = pltpu.roll(jnp.where(low, results[1], results[0]), LANES // 2, 1)
            outs.append(top / bottom)
        mixtures.append(jnp.concatenate(outs, axis=-1))
    mixture = jnp.concatenate(mixtures, axis=0).astype(BF16)
    copies[8].wait()
    hidden = (hidden.astype(F32) + dot(mixture, w_ao_scr[...])).astype(BF16)
    copies[9].wait()
    copies[10].wait()
    out_ref[...] = feed_forward(hidden, w_up_scr[...], w_down_scr[...])


def project_keys(rows, cols, half, me_ref, block, h_ref, w_k, w_v, cos_ref, sin_ref):
    wide = HEADS * half
    normed = rms_round(h_ref[...])
    left, right = turn_rows(rows, cols, wide, me_ref, block, dot(normed, w_k), 1.0, cos_ref, sin_ref)
    values = dot(normed, w_v).astype(BF16).reshape(rows, cols, 2 * wide)
    return left, right, values


def turn_rows(rows, cols, wide, me_ref, block, part, factor, cos_ref, sin_ref):
    scaled = part * (rms_scale(part) * factor)
    scaled = scaled.reshape(rows, cols, 2 * wide)
    first = lax.bitwise_xor(me_ref[0], block) * rows
    left, right = [], []
    for row in range(rows):
        cos, sin = cos_ref[pl.ds(first + row, 1), :], sin_ref[pl.ds(first + row, 1), :]
        a, c = scaled[row, :, :wide], scaled[row, :, wide:]
        left.append((a * cos - c * sin).astype(BF16))
        right.append((a * sin + c * cos).astype(BF16))
    return left, right


def mix_rows(rows, cols, half, q_left, q_right, keys, totals):
    wide = HEADS * half
    width = 2 * wide
    ids0 = lax.broadcasted_iota(jnp.int32, (width, width), 0)
    ids1 = lax.broadcasted_iota(jnp.int32, (width, width), 1)
    gather = jnp.where(ids0 // half == ids1 // half, 1.0, 0.0).astype(BF16)
    num_left, num_right, den = totals
    for two in range(0, len(keys), 2):
        prods = [q_left * k_l[None] + q_right * k_r[None] for k_l, k_r, _ in keys[two : two + 2]]
        score = dot(jnp.concatenate(prods, axis=-1).reshape(rows * cols, width), gather)
        weight = jnp.exp(score).reshape(rows, cols, width)
        for side, (_, _, value) in enumerate(keys[two : two + 2]):
            share = weight[..., side * wide : (side + 1) * wide]
            num_left += share * value[:, :wide].astype(F32)[None]
            num_right += share * value[:, wide:].astype(F32)[None]
            den += share
    return num_left, num_right, den


def all_keys(rows, cols, half, me_ref, blocks, h_refs, w_k, w_v, cos_ref, sin_ref):
    keys = []
    for block, h_ref in zip(blocks, h_refs):
        left, right, values = project_keys(rows, cols, half, me_ref, block, h_ref, w_k, w_v, cos_ref, sin_ref)
        keys += [(left[row], right[row], values[row]) for row in range(rows)]
    return keys


def level(moment):
    cosine = jnp.cos((moment / STEPS + 0.008) / 1.008 * math.pi / 2.0)
    return cosine * cosine


def early_kernel(blocks, rows, cols, me_ref, time_ref, *refs):
    h_refs = refs[: len(blocks)]
    w_qkv_ref, w_ao_ref, cos_ref, sin_ref = refs[len(blocks) : len(blocks) + 4]
    q_ref, left_ref, right_ref, den_ref, w_kv_ref, w_o_ref, coef_ref = refs[len(blocks) + 4 :]
    width = h_refs[0].shape[-1]
    head = width // HEADS
    half = head // 2
    wide = width // 2
    pick = shuffle_matrix(width, functools.partial(full_halves, width, half))
    w_q = dot(w_qkv_ref[1, :, :width], pick).astype(BF16)
    w_k = dot(w_qkv_ref[1, :, width : 2 * width], pick).astype(BF16)
    w_v = dot(w_qkv_ref[1, :, 2 * width :], pick).astype(BF16)
    w_kv_ref[:, :width] = w_k
    w_kv_ref[:, width:] = w_v
    w_o_ref[...] = lax.dot_general(
        pick, w_ao_ref[1], (((0,), (0,)), ((), ())), preferred_element_type=F32
    ).astype(BF16)
    part = dot(rms_round(h_refs[0][...]), w_q)
    left, right = turn_rows(rows, cols, wide, me_ref, 0, part, 1.0 / math.sqrt(head), cos_ref, sin_ref)
    q_left, q_right = jnp.stack(left), jnp.stack(right)
    q_ref[:, :, :wide] = q_left
    q_ref[:, :, wide:] = q_right
    keys = all_keys(rows, cols, half, me_ref, blocks, h_refs, w_k, w_v, cos_ref, sin_ref)
    totals = (jnp.zeros((rows, cols, wide), F32),) * 3
    left_ref[...], right_ref[...], den_ref[...] = mix_rows(rows, cols, half, q_left, q_right, keys, totals)
    moment = jnp.full((1, LANES), time_ref[0].astype(F32))
    now, after = level(moment), level(moment - STRIDE)
    keep = jnp.sqrt(1.0 - after) / jnp.sqrt(1.0 - now)
    coef_ref[0:1, :] = jnp.sqrt(after) - keep * jnp.sqrt(now)
    coef_ref[1:2, :] = keep


def late_kernel(blocks, rows, cols, chan, me_ref, own_ref, *refs):
    h_refs = refs[: len(blocks)]
    (
        q_ref, left_ref, right_ref, den_ref, w_kv_ref, w_o_ref, w_up_ref, w_down_ref, w_out_ref, cos_ref, sin_ref,
        out_ref, tok_scr,
    ) = refs[len(blocks) :]
    width = own_ref.shape[-1]
    half = width // HEADS // 2
    wide = width // 2
    keys = all_keys(
        rows, cols, half, me_ref, blocks, h_refs, w_kv_ref[:, :width], w_kv_ref[:, width:], cos_ref, sin_ref
    )
    left, right, den = mix_rows(
        rows, cols, half, q_ref[:, :, :wide], q_ref[:, :, wide:], keys,
        (left_ref[...], right_ref[...], den_ref[...]),
    )
    mixture = jnp.concatenate([left / den, right / den], axis=-1).astype(BF16)
    hidden = (own_ref[...].astype(F32) + dot(mixture.reshape(rows * cols, width), w_o_ref[...])).astype(BF16)
    hidden = feed_forward(hidden, w_up_ref[1], w_down_ref[1])
    tok_scr[:, :chan] = lax.dot_general(
        rms_round(hidden), w_out_ref[...], (((1,), (1,)), ((), ())), preferred_element_type=F32
    )
    pack_tokens(tok_scr, out_ref, rows, cols, chan)


def finish_kernel(count, dom_ref, anc_ref, coef_ref, *refs):
    states, preds = refs[:count], refs[count : 2 * count]
    new_state_ref, new_pred_ref, state_scr, sems = refs[2 * count :]
    pick = lax.bitwise_xor(anc_ref[dom_ref[0]], dom_ref[0])
    for k in range(count):

        def write(k=k):
            copy_pred = pltpu.make_async_copy(preds[k], new_pred_ref, sems.at[0])
            copy_pred.start()
            state_scr[...] = (
                coef_ref[0:1, 0:1][None] * preds[k][...].astype(F32)
                + coef_ref[1:2, 0:1][None] * states[k][...].astype(F32)
            ).astype(BF16)
            copy_state = pltpu.make_async_copy(state_scr, new_state_ref, sems.at[1])
            copy_state.start()
            copy_pred.wait()
            copy_state.wait()

        if count > 1:
            pl.when(pick == k)(write)
        else:
            write()


VMEM_SPEC = pl.BlockSpec(memory_space=pltpu.VMEM)
SMEM_SPEC = pl.BlockSpec(memory_space=pltpu.SMEM)
HBM_SPEC = pl.BlockSpec(memory_space=pltpu.HBM)


def cube(value, axis, size, bits):
    blocks = [value]
    step = bits // 2
    order = [0]
    while step:
        pairs = [(i, i ^ step) for i in range(size)]
        blocks = blocks + [lax.ppermute(b, axis, pairs) for b in blocks]
        order = order + [o ^ step for o in order]
        step //= 2
    return [blocks[order.index(b)] for b in range(bits)]


def kernel_call(body, name, operands, specs, outs, work, scratch=(), out_specs=None, limit=VMEM_LIMIT):
    single = not isinstance(outs, (list, tuple))
    if out_specs is None:
        out_specs = VMEM_SPEC if single else [VMEM_SPEC] * len(outs)
    return pl.pallas_call(
        body,
        out_shape=outs,
        in_specs=specs,
        out_specs=out_specs,
        scratch_shapes=list(scratch),
        compiler_params=pltpu.CompilerParams(vmem_limit_bytes=limit),
        cost_estimate=pl.CostEstimate(flops=work, bytes_accessed=0, transcendentals=0),
        name=name,
    )(*operands)


def make(mesh):
    n_dom, n_row = mesh.shape["dom"], mesh.shape["row"]

    def per_device(
        state, prev_pred, ancestors, timestep, w_in, w_time, w_qkv, w_attn_out, w_up, w_down, w_out
    ):
        rows, flat = state.shape[1], state.shape[2]
        chan, width = w_out.shape[1], w_out.shape[0]
        cols = flat // chan
        head = width // HEADS
        half = head // 2
        like = jax.ShapeDtypeStruct

        along = rotary_angles(cols, half, LANES)
        sign = np.where(np.arange(LANES) < LANES // 2, -1.0, 1.0)
        tables = [jnp.asarray(np.cos(along), F32), jnp.asarray(np.sin(along) * sign, F32)]
        scratch = [pltpu.SMEM(timestep.shape, jnp.int32)]
        for arr in (state, prev_pred, w_time, w_in):
            scratch.append(pltpu.VMEM(arr.shape, arr.dtype))
        for arr in (w_qkv, w_attn_out, w_up, w_down):
            scratch.append(pltpu.VMEM(arr.shape[1:], arr.dtype))
        for arr in tables:
            scratch.append(pltpu.VMEM(arr.shape, arr.dtype))
        scratch += [
            pltpu.VMEM((2 * rows, flat), F32),
            pltpu.VMEM((2 * rows * cols, LANES), F32),
            pltpu.SemaphoreType.DMA((11,)),
        ]
        hidden = kernel_call(
            functools.partial(row_kernel, rows, cols, chan), "row_block",
            (timestep, state, prev_pred, w_time, w_in, w_qkv, w_attn_out, w_up, w_down, *tables),
            [HBM_SPEC] * 11,
            like((rows * cols, width), BF16),
            5 * WORK_UNIT,
            scratch,
            limit=ROW_VMEM_LIMIT,
        )

        top = n_row // 2
        early = cube(hidden, "row", n_row, top)
        late = cube(lax.ppermute(hidden, "row", [(i, i ^ top) for i in range(n_row)]), "row", n_row, top)
        early_ids, late_ids = list(range(top)), list(range(top, n_row))
        down = rotary_angles(n_row * rows, half, width // 2)
        tables = [jnp.asarray(np.cos(down), F32), jnp.asarray(np.sin(down), F32)]
        me = lax.axis_index("row").astype(jnp.int32)[None]
        piece = like((rows, cols, width // 2), F32)
        *sums, w_kv, w_o, coefs = kernel_call(
            functools.partial(early_kernel, early_ids, rows, cols), "column_early",
            (me, timestep, *early, w_qkv, w_attn_out, *tables),
            [SMEM_SPEC] * 2 + [VMEM_SPEC] * (top + 4),
            [
                like((rows, cols, width), BF16), piece, piece, piece,
                like((width, 2 * width), BF16), like((width, width), BF16), like((2, LANES), F32),
            ],
            3 * WORK_UNIT,
        )
        own_pred = kernel_call(
            functools.partial(late_kernel, late_ids, rows, cols, chan), "column_late",
            (me, hidden, *late, *sums, w_kv, w_o, w_up, w_down, w_out.T, *tables),
            [SMEM_SPEC] + [VMEM_SPEC] * (top + 12),
            like((1, rows, flat), BF16),
            5 * WORK_UNIT,
            [pltpu.VMEM((rows * cols, LANES), F32)],
        )

        my_dom = lax.axis_index("dom").astype(jnp.int32)
        if n_dom & (n_dom - 1) == 0 and n_dom <= 8:
            state_late, _ = lax.optimization_barrier((state, hidden))
            states, preds = [
                [x] + [lax.ppermute(x, "dom", [(i, i ^ k) for i in range(n_dom)]) for k in range(1, n_dom)]
                for x in (state_late, own_pred)
            ]
        else:
            states, preds = [
                [lax.dynamic_index_in_dim(lax.all_gather(x, "dom"), ancestors[my_dom], 0, keepdims=False)]
                for x in (state, own_pred)
            ]
        shape = like(state.shape, BF16)
        return kernel_call(
            functools.partial(finish_kernel, len(preds)), "finish",
            (my_dom[None], ancestors, coefs, *states, *preds),
            [SMEM_SPEC] * 2 + [VMEM_SPEC] * (1 + 2 * len(preds)),
            (shape, shape),
            WORK_UNIT,
            [pltpu.VMEM(state.shape, BF16), pltpu.SemaphoreType.DMA((2,))],
            (HBM_SPEC, HBM_SPEC),
        )

    return per_device


def solution(mesh):
    spread = P(("group", "dom"), "row", None)
    return jax.shard_map(
        make(mesh),
        mesh=mesh,
        in_specs=(spread, spread, P("group"), P("group")) + (P(),) * 7,
        out_specs=(spread, spread),
        check_vma=False,
    )
```

time: 60.1 us -> 37.8 us (0.63)
  blocking collectives: 15.4 us -> 0 us
  local copies, waits for them, and re-layouts: 10.1 us -> 1.64 us
  starting transfers between devices: 7.77 us -> 11.9 us
  waiting for transfers between devices: 11.1 us -> 9.39 us
  Pallas kernels: 11.8 us -> 13.3 us
  between operations: 2.46 us -> 1.44 us
  other arithmetic: 0.85 us -> 0 us
    all_gather x1 -> x0, blocking collectives: 15.4 us -> none  [per_device(): all_states = lax.all_gather(state, 'dom', tiled=True)]
    unnamed x37 -> x22, local copies, waits for them, and re-layouts: 9.56 us -> 1.64 us
    ppermute x6 -> x9, starting transfers between devices: 7.77 us -> 11.9 us  [the longest x6 8.86 us: per_device(): lax.ppermute(x, 'dom', [(i, i ^ k) for i in range(n_dom)])]
    ppermute x6 -> x9, waiting for transfers between devices: 11.1 us -> 9.39 us  [the longest x6 7.26 us: per_device(): lax.ppermute(x, 'dom', [(i, i ^ k) for i in range(n_dom)])]
    pallas_call x3 -> x4, Pallas kernels: 11.8 us -> 13.3 us  [kernel_call(): pl.pallas_call(body, out_shape=outs, in_specs=specs, out_specs=out_specs,...]
    another operation x2 -> x0, other arithmetic: 0.79 us -> none  [the longest x1 0.72 us: per_device(): picks = jnp.stack([mine, choice]).astype(jnp.int32)]
  transfers between devices with their start and end apart: 6 -> 9, of which waited for: 3 -> 3; matrix products, arithmetic and copies ran while one was open for 5% -> 0% of each run, Pallas kernels for 0% -> 13%
where the time goes in v2:
time: 37.8 us; the launch traced here: 37.6 us
  Pallas kernels  13.3 us (35%)
  starting transfers between devices  11.9 us (31%)
  waiting for transfers between devices  9.39 us (25%)
  local copies, waits for them, and re-layouts  1.64 us (4%)
  between operations  1.44 us (4%)
    pallas_call x4, Pallas kernels, kernel_call(): pl.pallas_call(body, out_shape=outs, in_specs=specs, out_specs=out_specs,...  13.3 us
    ppermute x6, starting transfers between devices, per_device(): lax.ppermute(x, 'dom', [(i, i ^ k) for i in range(n_dom)])  8.86 us
    ppermute x6, waiting for transfers between devices, per_device(): lax.ppermute(x, 'dom', [(i, i ^ k) for i in range(n_dom)])  7.26 us
    ppermute x1, starting transfers between devices, per_device(): lax.ppermute(hidden, 'row', [(i, i ^ top) for i in range(n_row)])  3 us
    ppermute x1, waiting for transfers between devices, per_device(): lax.ppermute(hidden, 'row', [(i, i ^ top) for i in range(n_row)])  2.12 us
    unnamed x22, local copies, waits for them, and re-layouts  1.64 us
  transfers between devices with their start and end apart: 9, of which 3 were waited for; matrix products, arithmetic and copies ran while one was open for 0% of the time, Pallas kernels for 13%

profile of v2, /device:TPU:0, one launch (start us, length us, event | category | flops | bytes accessed | tf_op | source)
XLA Modules:
  0.0 37.6 jit_solution(9822012128041035636)
XLA Ops:
  1.3 0.0 copy-start.9
  1.3 0.0 copy-start.10
  1.3 7.0 %row_block.1.refs_0_.own_ref = bf16[512,256]{1,0:T(8,128)(2,1)} custom-call(s32[1]{0:T(128)S(6)} %copy.17.time_ref, bf16[1,4,10752]{2,1,0:T(4,128)(2,1)} %refs_0_, bf16[1,4,10752]{2,1,0:T(4,128)(2,1)} %prev_ref.1, bf16[256,256]{1,0:T(8,128)(2,1)} %w_time_ref.1, bf16[168,256]{1,0:T(8,128)(2,1)} %w_in_ref.1, bf16[2,256,768]{2,1,0:T(8,128)(2,1)} %refs_2_.1, ...), custom_call_target="tpu_custom_call" | custom-call | flops 5368709120 | tf_op jit(solution)/shard_map/row_block/pallas_call | solution.py:370
  8.3 3.0 %collective-permute-start.4 = (bf16[512,256]{1,0:T(8,128)(2,1)}, bf16[512,256]{1,0:T(8,128)(2,1)S(1)}, u32[]{:S(2)}, u32[]{:S(2)}) collective-permute-start(bf16[512,256]{1,0:T(8,128)(2,1)} %row_block.1.refs_0_.own_ref), channel_id=1, source_target_pairs={{0,2},{1,3},{2,0},{3,1},{4,6},{5,7},{6,4},{7,5},{8,10},{9,11},{10,... | collective-permute-start | bytes 786440 | tf_op jit(solution)/shard_map/ppermute | solution.py:422
  11.3 0.0 collective-permute-start
  11.3 1.6 %collective-permute-start.1 = (bf16[1,4,10752]{2,1,0:T(4,128)(2,1)S(1)}, bf16[1,4,10752]{2,1,0:T(4,128)(2,1)S(1)}, u32[]{:S(2)}, u32[]{:S(2)}) collective-permute-start(bf16[1,4,10752]{2,1,0:T(4,128)(2,1)S(1)} %copy-done.6), channel_id=1, source_target_pairs={{0,4},{4,0},{8,12},{12,8},{1,5},{5,1},{9,13},{13,9},{2,6},{6,2},{1... | collective-permute-start | bytes 258056 | tf_op jit(solution)/shard_map/ppermute | solution.py:451
  12.9 2.6 %collective-permute-start.2 = (bf16[1,4,10752]{2,1,0:T(4,128)(2,1)S(1)}, bf16[1,4,10752]{2,1,0:T(4,128)(2,1)S(1)}, u32[]{:S(2)}, u32[]{:S(2)}) collective-permute-start(bf16[1,4,10752]{2,1,0:T(4,128)(2,1)S(1)} %copy-done.6), channel_id=1, source_target_pairs={{0,8},{4,12},{8,0},{12,4},{1,9},{5,13},{9,1},{13,5},{2,10},{6,14},... | collective-permute-start | bytes 258056 | tf_op jit(solution)/shard_map/ppermute | solution.py:451
  15.5 0.2 collective-permute-start.3
  15.7 2.1 %collective-permute-done.4.refs_0_ = bf16[512,256]{1,0:T(8,128)(2,1)S(1)} collective-permute-done((bf16[512,256]{1,0:T(8,128)(2,1)}, bf16[512,256]{1,0:T(8,128)(2,1)S(1)}, u32[]{:S(2)}, u32[]{:S(2)}) %collective-permute-start.4) | collective-permute-done | bytes 262176 | tf_op jit(solution)/shard_map/ppermute | solution.py:422
  17.8 0.0 collective-permute-start.5
  17.8 0.0 collective-permute-done.refs_1_
  17.9 0.9 %copy-done.4 = bf16[512,256]{1,0:T(8,128)(2,1)S(1)} copy-done((bf16[512,256]{1,0:T(8,128)(2,1)S(1)}, bf16[512,256]{1,0:T(8,128)(2,1)}, u32[]{:S(2)}) %copy-start.4) | copy-done | bytes 262168
  18.8 1.7 %column_early.1 = (bf16[4,128,256]{2,1,0:T(8,128)(2,1)S(1)}, f32[4,128,128]{2,1,0:T(8,128)S(1)}, f32[4,128,128]{2,1,0:T(8,128)S(1)}, f32[4,128,128]{2,1,0:T(8,12...) custom-call(s32[1]{0:T(128)} %bitcast.1.me_ref, s32[1]{0:T(128)S(6)} %copy.17.time_ref, ...), custom_call_target="tpu_custom_call" | custom-call | flops 3221225472 | tf_op jit(solution)/shard_map/column_early/pallas_call | solution.py:370
  20.6 0.0 collective-permute-done.5.refs_1_
  20.6 3.3 %column_late.1.refs_4_ = bf16[1,4,10752]{2,1,0:T(4,128)(2,1)S(1)} custom-call(s32[1]{0:T(128)} %bitcast.1.me_ref, bf16[512,256]{1,0:T(8,128)(2,1)S(1)} %copy-done.5, bf16[512,256]{1,0:T(8,128)(2,1)S(1)} %collective-permute-done.4.refs_0_, bf16[512,256]{1,0:T(8,128)(2,1)S(1)} %collective-permute-done.5.refs_1_, ...), custom_call_target="tpu_custom_call" | custom-call | flops 5368709120 | tf_op jit(solution)/shard_map/column_late/pallas_call | solution.py:370
  23.9 1.9 %collective-permute-start.6 = (bf16[1,4,10752]{2,1,0:T(4,128)(2,1)S(1)}, bf16[1,4,10752]{2,1,0:T(4,128)(2,1)S(1)}, u32[]{:S(2)}, u32[]{:S(2)}) collective-permute-start(bf16[1,4,10752]{2,1,0:T(4,128)(2,1)S(1)} %column_late.1.refs_4_), channel_id=1, source_target_pairs={{0,4},{4,0},{8,12},{12,8},{1,5},{5,1},{9,13},{13,9},{2,6},{6,2},{1... | collective-permute-start | bytes 258056 | tf_op jit(solution)/shard_map/ppermute | solution.py:451
  25.8 2.6 %collective-permute-start.7 = (bf16[1,4,10752]{2,1,0:T(4,128)(2,1)S(1)}, bf16[1,4,10752]{2,1,0:T(4,128)(2,1)S(1)}, u32[]{:S(2)}, u32[]{:S(2)}) collective-permute-start(bf16[1,4,10752]{2,1,0:T(4,128)(2,1)S(1)} %column_late.1.refs_4_), channel_id=1, source_target_pairs={{0,8},{4,12},{8,0},{12,4},{1,9},{5,13},{9,1},{13,5},{2,10},{6,14},... | collective-permute-start | bytes 258056 | tf_op jit(solution)/shard_map/ppermute | solution.py:451
  28.4 0.0 collective-permute-done.1.refs_1_
  28.4 0.0 collective-permute-start.8
  28.4 0.0 collective-permute-done.2.refs_2_
  28.4 0.6 %collective-permute-done.6.refs_5_ = bf16[1,4,10752]{2,1,0:T(4,128)(2,1)S(1)} collective-permute-done((bf16[1,4,10752]{2,1,0:T(4,128)(2,1)S(1)}, bf16[1,4,10752]{2,1,0:T(4,128)(2,1)S(1)}, u32[]{:S(2)}, u32[]{:S(2)}) %collective-permute-start.6) | collective-permute-done | bytes 86048 | tf_op jit(solution)/shard_map/ppermute | solution.py:451
  29.0 6.7 %collective-permute-done.7.refs_6_ = bf16[1,4,10752]{2,1,0:T(4,128)(2,1)S(1)} collective-permute-done((bf16[1,4,10752]{2,1,0:T(4,128)(2,1)S(1)}, bf16[1,4,10752]{2,1,0:T(4,128)(2,1)S(1)}, u32[]{:S(2)}, u32[]{:S(2)}) %collective-permute-start.7) | collective-permute-done | bytes 86048 | tf_op jit(solution)/shard_map/ppermute | solution.py:451
  35.7 0.7 %copy-done.8 = s32[4]{0:T(128)S(1)} copy-done((s32[4]{0:T(128)S(1)}, s32[4]{0:T(128)}, u32[]{:S(2)}) %copy-start.8) | copy-done | bytes 40
  36.4 1.3 %finish.1 = (bf16[1,4,10752]{2,1,0:T(4,128)(2,1)}, bf16[1,4,10752]{2,1,0:T(4,128)(2,1)}) custom-call(s32[1]{0:T(128)} %bitcast.dom_ref, s32[4]{0:T(128)S(1)} %copy-done.8, f32[2,128]{1,0:T(2,128)S(1)} %get-tuple-element.10.coef_ref, bf16[1,4,10752]{2,1,0:T(4,128)(2,1)S(1)} %copy-done.6, bf16[1,4,10752]{2,1,0:T(4,128)(2,1)S(1)} %collective-permute-done.1.refs_1_, ...), custom_call_target="tpu_custom_call" | custom-call | flops 1073741824 | tf_op jit(solution)/shard_map/finish/pallas_call | solution.py:370
  (20 shorter events, 0.0 us)
Async XLA Ops:
  1.3 10.0 %copy-start.6 = (bf16[1,4,10752]{2,1,0:T(4,128)(2,1)S(1)}, bf16[1,4,10752]{2,1,0:T(4,128)(2,1)}, u32[]{:S(2)}) copy-start(bf16[1,4,10752]{2,1,0:T(4,128)(2,1)} %refs_0_) | copy-start | bytes 258052
  1.3 16.6 %copy-start.2 = (bf16[2,256,768]{2,1,0:T(8,128)(2,1)S(1)}, bf16[2,256,768]{2,1,0:T(8,128)(2,1)}, u32[]{:S(2)}) copy-start(bf16[2,256,768]{2,1,0:T(8,128)(2,1)} %refs_2_.1) | copy-start | bytes 2359300
  1.3 16.6 %copy-start.3 = (bf16[2,256,256]{2,1,0:T(8,128)(2,1)S(1)}, bf16[2,256,256]{2,1,0:T(8,128)(2,1)}, u32[]{:S(2)}) copy-start(bf16[2,256,256]{2,1,0:T(8,128)(2,1)} %refs_3_.1) | copy-start | bytes 786436
  1.3 16.6 %copy-start.9 = (f32[16,128]{1,0:T(8,128)S(1)}, f32[16,128]{1,0:T(8,128)}, u32[]{:S(2)}) copy-start(f32[16,128]{1,0:T(8,128)} %constant.17.clone.refs_4_.refs_11_) | copy-start | bytes 24580
  1.3 16.5 %copy-start.10 = (f32[16,128]{1,0:T(8,128)S(1)}, f32[16,128]{1,0:T(8,128)}, u32[]{:S(2)}) copy-start(f32[16,128]{1,0:T(8,128)} %constant.18.clone.refs_5_.refs_12_) | copy-start | bytes 24580
  8.3 9.5 %collective-permute-start.4 = (bf16[512,256]{1,0:T(8,128)(2,1)}, bf16[512,256]{1,0:T(8,128)(2,1)S(1)}, u32[]{:S(2)}, u32[]{:S(2)}) collective-permute-start(bf16[512,256]{1,0:T(8,128)(2,1)} %row_block.1.refs_0_.own_ref), channel_id=1, source_target_pairs={{0,2},{1,3},{2,0},{3,1},{4,6},{5,7},{6,4},{7,5},{8,10},{9,11},{10,... | collective-permute-start | bytes 786440 | tf_op jit(solution)/shard_map/ppermute | solution.py:422
  11.3 6.5 %collective-permute-start = (bf16[512,256]{1,0:T(8,128)(2,1)}, bf16[512,256]{1,0:T(8,128)(2,1)S(1)}, u32[]{:S(2)}, u32[]{:S(2)}) collective-permute-start(bf16[512,256]{1,0:T(8,128)(2,1)} %row_block.1.refs_0_.own_ref), channel_id=1, source_target_pairs={{0,1},{1,0},{2,3},{3,2},{4,5},{5,4},{6,7},{7,6},{8,9},{9,8},{10,11... | collective-permute-start | bytes 786440 | tf_op jit(solution)/shard_map/ppermute | solution.py:360
  11.3 17.1 %collective-permute-start.1 = (bf16[1,4,10752]{2,1,0:T(4,128)(2,1)S(1)}, bf16[1,4,10752]{2,1,0:T(4,128)(2,1)S(1)}, u32[]{:S(2)}, u32[]{:S(2)}) collective-permute-start(bf16[1,4,10752]{2,1,0:T(4,128)(2,1)S(1)} %copy-done.6), channel_id=1, source_target_pairs={{0,4},{4,0},{8,12},{12,8},{1,5},{5,1},{9,13},{13,9},{2,6},{6,2},{1... | collective-permute-start | bytes 258056 | tf_op jit(solution)/shard_map/ppermute | solution.py:451
  12.9 15.5 %collective-permute-start.2 = (bf16[1,4,10752]{2,1,0:T(4,128)(2,1)S(1)}, bf16[1,4,10752]{2,1,0:T(4,128)(2,1)S(1)}, u32[]{:S(2)}, u32[]{:S(2)}) collective-permute-start(bf16[1,4,10752]{2,1,0:T(4,128)(2,1)S(1)} %copy-done.6), channel_id=1, source_target_pairs={{0,8},{4,12},{8,0},{12,4},{1,9},{5,13},{9,1},{13,5},{2,10},{6,14},... | collective-permute-start | bytes 258056 | tf_op jit(solution)/shard_map/ppermute | solution.py:451
  15.5 12.9 %collective-permute-start.3 = (bf16[1,4,10752]{2,1,0:T(4,128)(2,1)S(1)}, bf16[1,4,10752]{2,1,0:T(4,128)(2,1)S(1)}, u32[]{:S(2)}, u32[]{:S(2)}) collective-permute-start(bf16[1,4,10752]{2,1,0:T(4,128)(2,1)S(1)} %copy-done.6), channel_id=1, source_target_pairs={{0,12},{4,8},{8,4},{12,0},{1,13},{5,9},{9,5},{13,1},{2,14},{6,10},... | collective-permute-start | bytes 258056 | tf_op jit(solution)/shard_map/ppermute | solution.py:451
  17.8 2.7 %collective-permute-start.5 = (bf16[512,256]{1,0:T(8,128)(2,1)S(1)}, bf16[512,256]{1,0:T(8,128)(2,1)S(1)}, u32[]{:S(2)}, u32[]{:S(2)}) collective-permute-start(bf16[512,256]{1,0:T(8,128)(2,1)S(1)} %collective-permute-done.4.refs_0_), channel_id=1, source_target_pairs={{0,1},{1,0},{2,3},{3,2},{4,5},{5,4},{6,7},{7,6},{8,9},{9,8},{10,11... | collective-permute-start | bytes 786440 | tf_op jit(solution)/shard_map/ppermute | solution.py:360
  17.9 1.0 %copy-start.4 = (bf16[512,256]{1,0:T(8,128)(2,1)S(1)}, bf16[512,256]{1,0:T(8,128)(2,1)}, u32[]{:S(2)}) copy-start(bf16[512,256]{1,0:T(8,128)(2,1)} %row_block.1.refs_0_.own_ref) | copy-start | bytes 786436
  18.8 1.7 %copy-start = (bf16[2,256,1024]{2,1,0:T(8,128)(2,1)S(1)}, bf16[2,256,1024]{2,1,0:T(8,128)(2,1)}, u32[]{:S(2)}) copy-start(bf16[2,256,1024]{2,1,0:T(8,128)(2,1)} %refs_8_.1) | copy-start | bytes 3145732
  18.8 1.7 %copy-start.1 = (bf16[2,1024,256]{2,1,0:T(8,128)(2,1)S(1)}, bf16[2,1024,256]{2,1,0:T(8,128)(2,1)}, u32[]{:S(2)}) copy-start(bf16[2,1024,256]{2,1,0:T(8,128)(2,1)} %refs_9_.1) | copy-start | bytes 3145732
  18.8 1.8 %copy-start.5 = (bf16[512,256]{1,0:T(8,128)(2,1)S(1)}, bf16[512,256]{1,0:T(8,128)(2,1)}, u32[]{:S(2)}) copy-start(bf16[512,256]{1,0:T(8,128)(2,1)} %row_block.1.refs_0_.own_ref) | copy-start | bytes 786436
  18.8 1.8 %copy-start.7 = (bf16[256,84]{0,1:T(8,128)(2,1)S(1)}, bf16[256,84]{0,1:T(8,128)(2,1)}, u32[]{:S(2)}) copy-start(bf16[256,84]{0,1:T(8,128)(2,1)} %param.25) | copy-start | bytes 129028
  23.9 5.1 %collective-permute-start.6 = (bf16[1,4,10752]{2,1,0:T(4,128)(2,1)S(1)}, bf16[1,4,10752]{2,1,0:T(4,128)(2,1)S(1)}, u32[]{:S(2)}, u32[]{:S(2)}) collective-permute-start(bf16[1,4,10752]{2,1,0:T(4,128)(2,1)S(1)} %column_late.1.refs_4_), channel_id=1, source_target_pairs={{0,4},{4,0},{8,12},{12,8},{1,5},{5,1},{9,13},{13,9},{2,6},{6,2},{1... | collective-permute-start | bytes 258056 | tf_op jit(solution)/shard_map/ppermute | solution.py:451
  25.8 9.9 %collective-permute-start.7 = (bf16[1,4,10752]{2,1,0:T(4,128)(2,1)S(1)}, bf16[1,4,10752]{2,1,0:T(4,128)(2,1)S(1)}, u32[]{:S(2)}, u32[]{:S(2)}) collective-permute-start(bf16[1,4,10752]{2,1,0:T(4,128)(2,1)S(1)} %column_late.1.refs_4_), channel_id=1, source_target_pairs={{0,8},{4,12},{8,0},{12,4},{1,9},{5,13},{9,1},{13,5},{2,10},{6,14},... | collective-permute-start | bytes 258056 | tf_op jit(solution)/shard_map/ppermute | solution.py:451
  28.4 7.3 %collective-permute-start.8 = (bf16[1,4,10752]{2,1,0:T(4,128)(2,1)S(1)}, bf16[1,4,10752]{2,1,0:T(4,128)(2,1)S(1)}, u32[]{:S(2)}, u32[]{:S(2)}) collective-permute-start(bf16[1,4,10752]{2,1,0:T(4,128)(2,1)S(1)} %column_late.1.refs_4_), channel_id=1, source_target_pairs={{0,12},{4,8},{8,4},{12,0},{1,13},{5,9},{9,5},{13,1},{2,14},{6,10},... | collective-permute-start | bytes 258056 | tf_op jit(solution)/shard_map/ppermute | solution.py:451
  35.7 0.7 %copy-start.8 = (s32[4]{0:T(128)S(1)}, s32[4]{0:T(128)}, u32[]{:S(2)}) copy-start(s32[4]{0:T(128)} %anc_ref.1) | copy-start | bytes 52

commit v3 on v2

--- a/solution.py
+++ b/solution.py
@@ -33,6 +33,17 @@
     return lax.rsqrt(jnp.mean(wide * wide, axis=-1, keepdims=True) + EPS)
 
 
+def rms_scale_mx(wide):
+    n = wide.shape[-1]
+    ones = jnp.full((n, n), 1.0 / n, BF16)
+    return lax.rsqrt(dot((wide * wide).astype(BF16), ones) + EPS)
+
+
+def rms_round_mx(values_in):
+    wide = values_in.astype(F32)
+    return (wide * rms_scale_mx(wide)).astype(BF16)
+
+
 def rms_round(values_in):
     wide = values_in.astype(F32)
     return (wide * rms_scale(wide)).astype(BF16)
@@ -43,7 +54,7 @@
 
 
 def feed_forward(hidden, w_up, w_down):
-    gated = gelu(dot(rms_round(hidden), w_up)).astype(BF16)
+    gated = gelu(dot(rms_round_mx(hidden), w_up)).astype(BF16)
     return (hidden.astype(F32) + dot(gated, w_down)).astype(BF16)
 
 
@@ -106,6 +117,11 @@
         out_ref[0, :, tile * LANES : (tile + 1) * LANES] = whole.astype(BF16)
 
 
+def level(moment):
+    cosine = jnp.cos((moment / STEPS + 0.008) / 1.008 * math.pi / 2.0)
+    return cosine * cosine
+
+
 def time_vector(moment, w_time):
     half = w_time.shape[0] // 2
     rates = jnp.exp(lane_ids((1, half)).astype(F32) * (-math.log(10000.0) / half))
@@ -120,67 +136,69 @@
 
 def row_kernel(
     rows, cols, chan,
-    time_ref, state_ref, prev_ref, w_time_ref, w_in_ref, w_qkv_ref, w_ao_ref, w_up_ref, w_down_ref, cos_ref, sin_ref,
-    out_ref,
-    time_scr, state_scr, prev_scr, w_time_scr, w_in_scr, w_qkv_scr, w_ao_scr, w_up_scr, w_down_scr, cos_scr, sin_scr,
+    time_ref, anc_ref, state_ref, prev_ref, w_time_ref, w_in_ref, w_qkv_ref, cos_ref, sin_ref, w_ao_ref, w_up_ref, w_down_ref, w_out_ref,
+    out_ref, state_scr, coef_ref, pick_ref, next_qkv_ref, next_ao_ref, next_up_ref, next_down_ref, next_out_ref,
+    anc_scr, prev_scr, w_time_scr, w_in_scr, w_qkv_scr, cos_scr, sin_scr, w_ao_scr, w_up_scr, w_down_scr,
     flat_scr, tok_scr, sems,
 ):
-    sources = (
-        time_ref, state_ref, prev_ref, w_time_ref, w_in_ref, w_qkv_ref.at[0], cos_ref, sin_ref,
-        w_ao_ref.at[0], w_up_ref.at[0], w_down_ref.at[0],
+    moves = (
+        (anc_ref, anc_scr), (state_ref, state_scr), (prev_ref, prev_scr), (w_time_ref, w_time_scr), (w_in_ref, w_in_scr),
+        (w_qkv_ref.at[0], w_qkv_scr), (cos_ref, cos_scr), (sin_ref, sin_scr),
+        (w_ao_ref.at[0], w_ao_scr), (w_up_ref.at[0], w_up_scr), (w_down_ref.at[0], w_down_scr),
+        (w_qkv_ref.at[1], next_qkv_ref), (w_ao_ref.at[1], next_ao_ref), (w_up_ref.at[1], next_up_ref),
+        (w_down_ref.at[1], next_down_ref), (w_out_ref, next_out_ref),
     )
-    targets = (
-        time_scr, state_scr, prev_scr, w_time_scr, w_in_scr, w_qkv_scr, cos_scr, sin_scr,
-        w_ao_scr, w_up_scr, w_down_scr,
-    )
-    copies = [pltpu.make_async_copy(s, t, sems.at[i]) for i, (s, t) in enumerate(zip(sources, targets))]
+    copies = [pltpu.make_async_copy(s, t, sems.at[i]) for i, (s, t) in enumerate(moves)]
     for copy in copies:
         copy.start()
     width = out_ref.shape[-1]
     head = width // HEADS
     half = head // 2
-    copies[0].wait()
-    copies[1].wait()
+    copies[3].wait()
+    offset_vec = time_vector(time_ref[0].astype(F32), w_time_scr[...])
+    for c in copies[1:3] + copies[4:11]:
+        c.wait()
     flat_scr[:rows, :] = state_scr[0].astype(F32)
-    copies[2].wait()
     flat_scr[rows:, :] = prev_scr[0].astype(F32)
     unpack_tokens(flat_scr, tok_scr, cols, chan)
     count = rows * cols
-    copies[3].wait()
-    offset_vec = time_vector(time_scr[0].astype(F32), w_time_scr[...])
-    copies[4].wait()
     w_in = w_in_scr[...].astype(F32)
     blank = jnp.zeros((LANES - chan, width), F32)
     w_state = jnp.concatenate([w_in[:chan], blank], axis=0).astype(BF16)
     w_prev = jnp.concatenate([w_in[chan:], blank], axis=0).astype(BF16)
-    hidden = dot(tok_scr[:count].astype(BF16), w_state) + dot(tok_scr[count:].astype(BF16), w_prev)
+    hidden = dot(jnp.concatenate([tok_scr[:count].astype(BF16), tok_scr[count:].astype(BF16)], axis=-1), jnp.concatenate([w_state, w_prev], axis=0))
     hidden = (hidden + offset_vec).astype(BF16)
 
-    copies[5].wait()
-    copies[6].wait()
-    copies[7].wait()
     pick = shuffle_matrix(width, functools.partial(tile_halves, half))
     w_q = dot(w_qkv_scr[:, :width], pick).astype(BF16)
     w_k = dot(w_qkv_scr[:, width : 2 * width], pick).astype(BF16)
     w_v = w_qkv_scr[:, 2 * width :]
-    normed = rms_round(hidden)
+    normed = rms_round_mx(hidden)
     cos, sin = cos_scr[...], sin_scr[...]
     lane = lane_ids((cols, LANES))
     per_tile = LANES // head
     pair = per_tile // 2
 
+    def swap_halves(weight):
+        parts = []
+        for t in range(width // LANES):
+            mid = t * LANES + LANES // 2
+            parts += [weight[:, mid : (t + 1) * LANES], weight[:, t * LANES : mid]]
+        return jnp.concatenate(parts, axis=-1)
+
     def spin(part):
-        scaled = part * rms_scale(part)
+        plain = dot(normed, part)
+        swapped = dot(normed, swap_halves(part))
+        factor = rms_scale_mx(plain)
         tiles = []
         for t in range(width // LANES):
-            piece = scaled[:, t * LANES : (t + 1) * LANES].reshape(rows, cols, LANES)
-            swapped = pltpu.roll(piece, LANES // 2, 2)
-            tiles.append(piece * cos[None] + swapped * sin[None])
+            piece, other, scale = (x[:, t * LANES : (t + 1) * LANES].reshape(rows, cols, LANES) for x in (plain, swapped, factor))
+            tiles.append((piece * cos[None] + other * sin[None]) * scale)
         return tiles
 
     scale = 1.0 / math.sqrt(head)
-    queries = [(x * scale).astype(BF16) for x in spin(dot(normed, w_q))]
-    keys = [x.astype(BF16) for x in spin(dot(normed, w_k))]
+    queries = [(x * scale).astype(BF16) for x in spin(w_q)]
+    keys = [x.astype(BF16) for x in spin(w_k)]
     values = dot(normed, w_v).astype(BF16).reshape(rows, cols, width)
 
     mixtures = []
@@ -205,25 +223,30 @@
             outs.append(top / bottom)
         mixtures.append(jnp.concatenate(outs, axis=-1))
     mixture = jnp.concatenate(mixtures, axis=0).astype(BF16)
-    copies[8].wait()
     hidden = (hidden.astype(F32) + dot(mixture, w_ao_scr[...])).astype(BF16)
-    copies[9].wait()
-    copies[10].wait()
     out_ref[...] = feed_forward(hidden, w_up_scr[...], w_down_scr[...])
-
-
-def project_keys(rows, cols, half, me_ref, block, h_ref, w_k, w_v, cos_ref, sin_ref):
+    moment = jnp.full((1, LANES), time_ref[0].astype(F32))
+    now, after = level(moment), level(moment - STRIDE)
+    keep = jnp.sqrt(1.0 - after) / jnp.sqrt(1.0 - now)
+    coef_ref[0:1, :] = jnp.sqrt(after) - keep * jnp.sqrt(now)
+    coef_ref[1:2, :] = keep
+    for copy in copies[11:] + copies[:1]:
+        copy.wait()
+    pick_ref[0] = anc_scr[lax.axis_index("dom")]
+
+
+def project_keys(rows, cols, half, block, h_ref, w_k, w_v, cos_ref, sin_ref):
     wide = HEADS * half
     normed = rms_round(h_ref[...])
-    left, right = turn_rows(rows, cols, wide, me_ref, block, dot(normed, w_k), 1.0, cos_ref, sin_ref)
+    left, right = turn_rows(rows, cols, wide, block, dot(normed, w_k), 1.0, cos_ref, sin_ref)
     values = dot(normed, w_v).astype(BF16).reshape(rows, cols, 2 * wide)
     return left, right, values
 
 
-def turn_rows(rows, cols, wide, me_ref, block, part, factor, cos_ref, sin_ref):
+def turn_rows(rows, cols, wide, block, part, factor, cos_ref, sin_ref):
     scaled = part * (rms_scale(part) * factor)
     scaled = scaled.reshape(rows, cols, 2 * wide)
-    first = lax.bitwise_xor(me_ref[0], block) * rows
+    first = lax.bitwise_xor(lax.axis_index("row"), block) * rows
     left, right = [], []
     for row in range(rows):
         cos, sin = cos_ref[pl.ds(first + row, 1), :], sin_ref[pl.ds(first + row, 1), :]
@@ -252,52 +275,42 @@
     return num_left, num_right, den
 
 
-def all_keys(rows, cols, half, me_ref, blocks, h_refs, w_k, w_v, cos_ref, sin_ref):
+def all_keys(rows, cols, half, blocks, h_refs, w_k, w_v, cos_ref, sin_ref):
     keys = []
     for block, h_ref in zip(blocks, h_refs):
-        left, right, values = project_keys(rows, cols, half, me_ref, block, h_ref, w_k, w_v, cos_ref, sin_ref)
+        left, right, values = project_keys(rows, cols, half, block, h_ref, w_k, w_v, cos_ref, sin_ref)
         keys += [(left[row], right[row], values[row]) for row in range(rows)]
     return keys
 
 
-def level(moment):
-    cosine = jnp.cos((moment / STEPS + 0.008) / 1.008 * math.pi / 2.0)
-    return cosine * cosine
-
-
-def early_kernel(blocks, rows, cols, me_ref, time_ref, *refs):
+def early_kernel(blocks, rows, cols, *refs):
     h_refs = refs[: len(blocks)]
     w_qkv_ref, w_ao_ref, cos_ref, sin_ref = refs[len(blocks) : len(blocks) + 4]
-    q_ref, left_ref, right_ref, den_ref, w_kv_ref, w_o_ref, coef_ref = refs[len(blocks) + 4 :]
+    q_ref, left_ref, right_ref, den_ref, w_kv_ref, w_o_ref = refs[len(blocks) + 4 :]
     width = h_refs[0].shape[-1]
     head = width // HEADS
     half = head // 2
     wide = width // 2
     pick = shuffle_matrix(width, functools.partial(full_halves, width, half))
-    w_q = dot(w_qkv_ref[1, :, :width], pick).astype(BF16)
-    w_k = dot(w_qkv_ref[1, :, width : 2 * width], pick).astype(BF16)
-    w_v = dot(w_qkv_ref[1, :, 2 * width :], pick).astype(BF16)
+    w_q = dot(w_qkv_ref[:, :width], pick).astype(BF16)
+    w_k = dot(w_qkv_ref[:, width : 2 * width], pick).astype(BF16)
+    w_v = dot(w_qkv_ref[:, 2 * width :], pick).astype(BF16)
     w_kv_ref[:, :width] = w_k
     w_kv_ref[:, width:] = w_v
     w_o_ref[...] = lax.dot_general(
-        pick, w_ao_ref[1], (((0,), (0,)), ((), ())), preferred_element_type=F32
+        pick, w_ao_ref[...], (((0,), (0,)), ((), ())), preferred_element_type=F32
     ).astype(BF16)
     part = dot(rms_round(h_refs[0][...]), w_q)
-    left, right = turn_rows(rows, cols, wide, me_ref, 0, part, 1.0 / math.sqrt(head), cos_ref, sin_ref)
+    left, right = turn_rows(rows, cols, wide, 0, part, 1.0 / math.sqrt(head), cos_ref, sin_ref)
     q_left, q_right = jnp.stack(left), jnp.stack(right)
     q_ref[:, :, :wide] = q_left
     q_ref[:, :, wide:] = q_right
-    keys = all_keys(rows, cols, half, me_ref, blocks, h_refs, w_k, w_v, cos_ref, sin_ref)
+    keys = all_keys(rows, cols, half, blocks, h_refs, w_k, w_v, cos_ref, sin_ref)
     totals = (jnp.zeros((rows, cols, wide), F32),) * 3
     left_ref[...], right_ref[...], den_ref[...] = mix_rows(rows, cols, half, q_left, q_right, keys, totals)
-    moment = jnp.full((1, LANES), time_ref[0].astype(F32))
-    now, after = level(moment), level(moment - STRIDE)
-    keep = jnp.sqrt(1.0 - after) / jnp.sqrt(1.0 - now)
-    coef_ref[0:1, :] = jnp.sqrt(after) - keep * jnp.sqrt(now)
-    coef_ref[1:2, :] = keep
-
-
-def late_kernel(blocks, rows, cols, chan, me_ref, own_ref, *refs):
+
+
+def late_kernel(blocks, rows, cols, chan, own_ref, *refs):
     h_refs = refs[: len(blocks)]
     (
         q_ref, left_ref, right_ref, den_ref, w_kv_ref, w_o_ref, w_up_ref, w_down_ref, w_out_ref, cos_ref, sin_ref,
@@ -307,7 +320,7 @@
     half = width // HEADS // 2
     wide = width // 2
     keys = all_keys(
-        rows, cols, half, me_ref, blocks, h_refs, w_kv_ref[:, :width], w_kv_ref[:, width:], cos_ref, sin_ref
+        rows, cols, half, blocks, h_refs, w_kv_ref[:, :width], w_kv_ref[:, width:], cos_ref, sin_ref
     )
     left, right, den = mix_rows(
         rows, cols, half, q_ref[:, :, :wide], q_ref[:, :, wide:], keys,
@@ -315,20 +328,21 @@
     )
     mixture = jnp.concatenate([left / den, right / den], axis=-1).astype(BF16)
     hidden = (own_ref[...].astype(F32) + dot(mixture.reshape(rows * cols, width), w_o_ref[...])).astype(BF16)
-    hidden = feed_forward(hidden, w_up_ref[1], w_down_ref[1])
+    hidden = feed_forward(hidden, w_up_ref[...], w_down_ref[...])
     tok_scr[:, :chan] = lax.dot_general(
         rms_round(hidden), w_out_ref[...], (((1,), (1,)), ((), ())), preferred_element_type=F32
     )
     pack_tokens(tok_scr, out_ref, rows, cols, chan)
 
 
-def finish_kernel(count, dom_ref, anc_ref, coef_ref, *refs):
+def finish_kernel(turn, pick_ref, coef_ref, *refs):
+    count = len(turn)
     states, preds = refs[:count], refs[count : 2 * count]
     new_state_ref, new_pred_ref, state_scr, sems = refs[2 * count :]
-    pick = lax.bitwise_xor(anc_ref[dom_ref[0]], dom_ref[0])
-    for k in range(count):
-
-        def write(k=k):
+    pick = lax.bitwise_xor(pick_ref[0], lax.axis_index("dom"))
+    for place, k in enumerate(turn):
+
+        def write(k=place):
             copy_pred = pltpu.make_async_copy(preds[k], new_pred_ref, sems.at[0])
             copy_pred.start()
             state_scr[...] = (
@@ -395,72 +409,81 @@
         along = rotary_angles(cols, half, LANES)
         sign = np.where(np.arange(LANES) < LANES // 2, -1.0, 1.0)
         tables = [jnp.asarray(np.cos(along), F32), jnp.asarray(np.sin(along) * sign, F32)]
-        scratch = [pltpu.SMEM(timestep.shape, jnp.int32)]
-        for arr in (state, prev_pred, w_time, w_in):
-            scratch.append(pltpu.VMEM(arr.shape, arr.dtype))
-        for arr in (w_qkv, w_attn_out, w_up, w_down):
-            scratch.append(pltpu.VMEM(arr.shape[1:], arr.dtype))
-        for arr in tables:
-            scratch.append(pltpu.VMEM(arr.shape, arr.dtype))
-        scratch += [
-            pltpu.VMEM((2 * rows, flat), F32),
-            pltpu.VMEM((2 * rows * cols, LANES), F32),
-            pltpu.SemaphoreType.DMA((11,)),
-        ]
-        hidden = kernel_call(
+        like_of = lambda arr: like(arr.shape, arr.dtype)
+        block_of = lambda arr: like(arr.shape[1:], arr.dtype)
+        vmem = lambda arr: pltpu.VMEM(arr.shape, arr.dtype)
+        block_vmem = lambda arr: pltpu.VMEM(arr.shape[1:], arr.dtype)
+        my_dom = lax.axis_index("dom").astype(jnp.int32)
+        inputs = (
+            timestep, ancestors, state, prev_pred, w_time, w_in, w_qkv, *tables, w_attn_out, w_up, w_down, w_out.T,
+        )
+        hidden, state_out, coefs, pick, *weights = kernel_call(
             functools.partial(row_kernel, rows, cols, chan), "row_block",
-            (timestep, state, prev_pred, w_time, w_in, w_qkv, w_attn_out, w_up, w_down, *tables),
-            [HBM_SPEC] * 11,
-            like((rows * cols, width), BF16),
+            (timestep, *[pltpu.with_memory_space_constraint(x, pltpu.HBM) for x in inputs[1:]]),
+            [SMEM_SPEC] + [HBM_SPEC] * (len(inputs) - 1),
+            [
+                like((rows * cols, width), BF16), like_of(state), like((2, LANES), F32), like((1,), jnp.int32),
+                block_of(w_qkv), block_of(w_attn_out), block_of(w_up), block_of(w_down), like_of(w_out.T),
+            ],
             5 * WORK_UNIT,
-            scratch,
-            limit=ROW_VMEM_LIMIT,
+            [
+                pltpu.SMEM(ancestors.shape, jnp.int32),
+                vmem(prev_pred), vmem(w_time), vmem(w_in), block_vmem(w_qkv), vmem(tables[0]), vmem(tables[1]),
+                block_vmem(w_attn_out), block_vmem(w_up), block_vmem(w_down),
+                pltpu.VMEM((2 * rows, flat), F32),
+                pltpu.VMEM((2 * rows * cols, LANES), F32),
+                pltpu.SemaphoreType.DMA((16,)),
+            ],
+            [VMEM_SPEC] * 3 + [SMEM_SPEC] + [VMEM_SPEC] * 5,
         )
+        w_qkv1, w_ao1, w_up1, w_down1, w_out1 = weights
 
         top = n_row // 2
         early = cube(hidden, "row", n_row, top)
-        late = cube(lax.ppermute(hidden, "row", [(i, i ^ top) for i in range(n_row)]), "row", n_row, top)
+        across = lax.ppermute(hidden, "row", [(i, i ^ top) for i in range(n_row)])
         early_ids, late_ids = list(range(top)), list(range(top, n_row))
         down = rotary_angles(n_row * rows, half, width // 2)
         tables = [jnp.asarray(np.cos(down), F32), jnp.asarray(np.sin(down), F32)]
-        me = lax.axis_index("row").astype(jnp.int32)[None]
         piece = like((rows, cols, width // 2), F32)
-        *sums, w_kv, w_o, coefs = kernel_call(
+        *sums, w_kv, w_o = kernel_call(
             functools.partial(early_kernel, early_ids, rows, cols), "column_early",
-            (me, timestep, *early, w_qkv, w_attn_out, *tables),
-            [SMEM_SPEC] * 2 + [VMEM_SPEC] * (top + 4),
+            (*early, w_qkv1, w_ao1, *tables),
+            [VMEM_SPEC] * (top + 4),
             [
                 like((rows, cols, width), BF16), piece, piece, piece,
-                like((width, 2 * width), BF16), like((width, width), BF16), like((2, LANES), F32),
+                like((width, 2 * width), BF16), like((width, width), BF16),
             ],
             3 * WORK_UNIT,
         )
+        late = cube(across, "row", n_row, top)
         own_pred = kernel_call(
             functools.partial(late_kernel, late_ids, rows, cols, chan), "column_late",
-            (me, hidden, *late, *sums, w_kv, w_o, w_up, w_down, w_out.T, *tables),
-            [SMEM_SPEC] + [VMEM_SPEC] * (top + 12),
+            (hidden, *late, *sums, w_kv, w_o, w_up1, w_down1, w_out1, *tables),
+            [VMEM_SPEC] * (top + 12),
             like((1, rows, flat), BF16),
             5 * WORK_UNIT,
             [pltpu.VMEM((rows * cols, LANES), F32)],
         )
 
-        my_dom = lax.axis_index("dom").astype(jnp.int32)
         if n_dom & (n_dom - 1) == 0 and n_dom <= 8:
-            state_late, _ = lax.optimization_barrier((state, hidden))
-            states, preds = [
-                [x] + [lax.ppermute(x, "dom", [(i, i ^ k) for i in range(n_dom)]) for k in range(1, n_dom)]
-                for x in (state_late, own_pred)
-            ]
+
+            def spread(value):
+                got = [lax.ppermute(value, "dom", [(i, i ^ k) for i in range(n_dom)]) for k in range(n_dom - 1, 0, -1)]
+                return [value] + got[::-1]
         else:
-            states, preds = [
-                [lax.dynamic_index_in_dim(lax.all_gather(x, "dom"), ancestors[my_dom], 0, keepdims=False)]
-                for x in (state, own_pred)
-            ]
+
+            def spread(value):
+                every = lax.all_gather(value, "dom")
+                return [lax.dynamic_index_in_dim(every, ancestors[my_dom], 0, keepdims=False)]
+
+        states, preds = spread(state_out), spread(own_pred)
         shape = like(state.shape, BF16)
+        turn = list(range(0, len(preds), 2)) + list(range(len(preds) - 1, 0, -2))
+        states, preds = [[x[i] for i in turn] for x in (states, preds)]
         return kernel_call(
-            functools.partial(finish_kernel, len(preds)), "finish",
-            (my_dom[None], ancestors, coefs, *states, *preds),
-            [SMEM_SPEC] * 2 + [VMEM_SPEC] * (1 + 2 * len(preds)),
+            functools.partial(finish_kernel, turn), "finish",
+            (pick, coefs, *states, *preds),
+            [SMEM_SPEC] + [VMEM_SPEC] * (1 + 2 * len(preds)),
             (shape, shape),
             WORK_UNIT,
             [pltpu.VMEM(state.shape, BF16), pltpu.SemaphoreType.DMA((2,))],

time: 37.8 us -> 34 us (0.90)
  local copies, waits for them, and re-layouts: 1.64 us -> 0.01 us
  Pallas kernels: 13.3 us -> 12 us
  waiting for transfers between devices: 9.39 us -> 8.83 us
    unnamed x22 -> x4, local copies, waits for them, and re-layouts: 1.64 us -> 0.01 us
    pallas_call x4, Pallas kernels: 13.3 us -> 12 us  [kernel_call(): pl.pallas_call(body, out_shape=outs, in_specs=specs, out_specs=out_specs,...]
    ppermute x7, waiting for transfers between devices: 9.38 us -> 8.83 us  [the longest x6 6.69 us: spread(): lax.ppermute(value, 'dom', [(i, i ^ k) for i in range(n_dom)])]
  transfers between devices with their start and end apart: 9 -> 9, of which waited for: 3 -> 3; matrix products, arithmetic and copies ran while one was open for 0% -> 0% of each run, Pallas kernels for 13% -> 15%
where the time goes in v3:
time: 34 us; the launch traced here: 33.8 us
  Pallas kernels  12 us (35%)
  starting transfers between devices  11.7 us (34%)
  waiting for transfers between devices  8.83 us (26%)
  between operations  1.34 us (4%)
    pallas_call x4, Pallas kernels, kernel_call(): pl.pallas_call(body, out_shape=outs, in_specs=specs, out_specs=out_specs,...  12 us
    ppermute x6, starting transfers between devices, spread(): lax.ppermute(value, 'dom', [(i, i ^ k) for i in range(n_dom)])  8.65 us
    ppermute x6, waiting for transfers between devices, spread(): lax.ppermute(value, 'dom', [(i, i ^ k) for i in range(n_dom)])  6.69 us
    ppermute x1, starting transfers between devices, per_device(): across = lax.ppermute(hidden, 'row', [(i, i ^ top) for i in range(n_row)])  3 us
    ppermute x1, waiting for transfers between devices, per_device(): across = lax.ppermute(hidden, 'row', [(i, i ^ top) for i in range(n_row)])  2.14 us
  transfers between devices with their start and end apart: 9, of which 3 were waited for; matrix products, arithmetic and copies ran while one was open for 0% of the time, Pallas kernels for 15%

profile of v3, /device:TPU:0, one launch (start us, length us, event | category | flops | bytes accessed | tf_op | source)
XLA Modules:
  0.0 33.8 jit_solution(16980697801041945243)
XLA Ops:
  1.3 0.0 copy-start
  1.3 0.0 copy-start.1
  1.3 5.5 %row_block.1 = (bf16[512,256]{1,0:T(8,128)(2,1)S(1)}, bf16[1,4,10752]{2,1,0:T(4,128)(2,1)S(1)}, f32[2,128]{1,0:T(2,128)S(1)}, s32[1]{0:T(128)}, bf16[256,768]{1,...) custom-call(s32[1]{0:T(128)S(6)} %copy.17.time_ref, ...), custom_call_target="tpu_custom_call" | custom-call | flops 5368709120 | tf_op jit(solution)/shard_map/row_block/pallas_call | solution.py:384
  6.8 3.0 %collective-permute-start.3 = (bf16[512,256]{1,0:T(8,128)(2,1)S(1)}, bf16[512,256]{1,0:T(8,128)(2,1)S(1)}, u32[]{:S(2)}, u32[]{:S(2)}) collective-permute-start(bf16[512,256]{1,0:T(8,128)(2,1)S(1)} %get-tuple-element.20.refs_0_.own_ref), channel_id=1, source_target_pairs={{0,2},{1,3},{2,0},{3,1},{4,6},{5,7},{6,4},{7,5},{8,10},{9,11},{10,... | collective-permute-start | bytes 786440 | tf_op jit(solution)/shard_map/ppermute | solution.py:443
  9.8 0.0 collective-permute-start.5
  9.8 2.6 %collective-permute-start = (bf16[1,4,10752]{2,1,0:T(4,128)(2,1)S(1)}, bf16[1,4,10752]{2,1,0:T(4,128)(2,1)S(1)}, u32[]{:S(2)}, u32[]{:S(2)}) collective-permute-start(bf16[1,4,10752]{2,1,0:T(4,128)(2,1)S(1)} %get-tuple-element.19.refs_0_), channel_id=1, source_target_pairs={{0,8},{4,12},{8,0},{12,4},{1,9},{5,13},{9,1},{13,5},{2,10},{6,14},... | collective-permute-start | bytes 258056 | tf_op jit(solution)/shard_map/ppermute | solution.py:471
  12.4 1.3 %collective-permute-start.1 = (bf16[1,4,10752]{2,1,0:T(4,128)(2,1)S(1)}, bf16[1,4,10752]{2,1,0:T(4,128)(2,1)S(1)}, u32[]{:S(2)}, u32[]{:S(2)}) collective-permute-start(bf16[1,4,10752]{2,1,0:T(4,128)(2,1)S(1)} %get-tuple-element.19.refs_0_), channel_id=1, source_target_pairs={{0,12},{4,8},{8,4},{12,0},{1,13},{5,9},{9,5},{13,1},{2,14},{6,10},... | collective-permute-start | bytes 258056 | tf_op jit(solution)/shard_map/ppermute | solution.py:471
  13.8 0.2 collective-permute-start.2
  14.0 2.1 %collective-permute-done.3.refs_0_ = bf16[512,256]{1,0:T(8,128)(2,1)S(1)} collective-permute-done((bf16[512,256]{1,0:T(8,128)(2,1)S(1)}, bf16[512,256]{1,0:T(8,128)(2,1)S(1)}, u32[]{:S(2)}, u32[]{:S(2)}) %collective-permute-start.3) | collective-permute-done | bytes 262176 | tf_op jit(solution)/shard_map/ppermute | solution.py:443
  16.1 0.0 collective-permute-start.4
  16.1 0.0 collective-permute-done.5.refs_1_
  16.2 1.7 %column_early.1 = (bf16[4,128,256]{2,1,0:T(8,128)(2,1)S(1)}, f32[4,128,128]{2,1,0:T(8,128)S(1)}, f32[4,128,128]{2,1,0:T(8,128)S(1)}, f32[4,128,128]{2,1,0:T(8,12...) custom-call(bf16[512,256]{1,0:T(8,128)(2,1)S(1)} %get-tuple-element.20.refs_0_.own_ref, ...), custom_call_target="tpu_custom_call" | custom-call | flops 3221225472 | tf_op jit(solution)/shard_map/column_early/pallas_call | solution.py:384
  17.8 0.0 collective-permute-done.4.refs_1_
  17.8 3.4 %column_late.1.refs_4_ = bf16[1,4,10752]{2,1,0:T(4,128)(2,1)S(1)} custom-call(bf16[512,256]{1,0:T(8,128)(2,1)S(1)} %get-tuple-element.20.refs_0_.own_ref, bf16[512,256]{1,0:T(8,128)(2,1)S(1)} %collective-permute-done.3.refs_0_, bf16[512,256]{1,0:T(8,128)(2,1)S(1)} %collective-permute-done.4.refs_1_, bf16[4,128,256]{2,1,0:T(8,128)(2,1)S(1)} %get-tuple-element.23.refs_2_, ...), custom_call_target="tpu_custom_call" | custom-call | flops 5368709120 | tf_op jit(solution)/shard_map/column_late/pallas_call | solution.py:384
  21.3 2.9 %collective-permute-start.6 = (bf16[1,4,10752]{2,1,0:T(4,128)(2,1)S(1)}, bf16[1,4,10752]{2,1,0:T(4,128)(2,1)S(1)}, u32[]{:S(2)}, u32[]{:S(2)}) collective-permute-start(bf16[1,4,10752]{2,1,0:T(4,128)(2,1)S(1)} %column_late.1.refs_4_), channel_id=1, source_target_pairs={{0,8},{4,12},{8,0},{12,4},{1,9},{5,13},{9,1},{13,5},{2,10},{6,14},... | collective-permute-start | bytes 258056 | tf_op jit(solution)/shard_map/ppermute | solution.py:471
  24.2 1.3 %collective-permute-start.7 = (bf16[1,4,10752]{2,1,0:T(4,128)(2,1)S(1)}, bf16[1,4,10752]{2,1,0:T(4,128)(2,1)S(1)}, u32[]{:S(2)}, u32[]{:S(2)}) collective-permute-start(bf16[1,4,10752]{2,1,0:T(4,128)(2,1)S(1)} %column_late.1.refs_4_), channel_id=1, source_target_pairs={{0,12},{4,8},{8,4},{12,0},{1,13},{5,9},{9,5},{13,1},{2,14},{6,10},... | collective-permute-start | bytes 258056 | tf_op jit(solution)/shard_map/ppermute | solution.py:471
  25.5 0.0 collective-permute-done.refs_1_
  25.5 0.2 collective-permute-start.8
  25.8 0.0 collective-permute-done.1.refs_2_
  25.8 0.0 collective-permute-done.2.refs_3_
  25.8 5.6 %collective-permute-done.6.refs_5_ = bf16[1,4,10752]{2,1,0:T(4,128)(2,1)S(1)} collective-permute-done((bf16[1,4,10752]{2,1,0:T(4,128)(2,1)S(1)}, bf16[1,4,10752]{2,1,0:T(4,128)(2,1)S(1)}, u32[]{:S(2)}, u32[]{:S(2)}) %collective-permute-start.6) | collective-permute-done | bytes 86048 | tf_op jit(solution)/shard_map/ppermute | solution.py:471
  31.4 0.0 collective-permute-done.7.refs_6_
  31.4 1.1 %collective-permute-done.8.refs_7_ = bf16[1,4,10752]{2,1,0:T(4,128)(2,1)S(1)} collective-permute-done((bf16[1,4,10752]{2,1,0:T(4,128)(2,1)S(1)}, bf16[1,4,10752]{2,1,0:T(4,128)(2,1)S(1)}, u32[]{:S(2)}, u32[]{:S(2)}) %collective-permute-start.8) | collective-permute-done | bytes 86048 | tf_op jit(solution)/shard_map/ppermute | solution.py:471
  32.4 1.4 %finish.1 = (bf16[1,4,10752]{2,1,0:T(4,128)(2,1)}, bf16[1,4,10752]{2,1,0:T(4,128)(2,1)}) custom-call(s32[1]{0:T(128)} %get-tuple-element.17.pick_ref, f32[2,128]{1,0:T(2,128)S(1)} %get-tuple-element.18.coef_ref, bf16[1,4,10752]{2,1,0:T(4,128)(2,1)S(1)} %get-tuple-element.19.refs_0_, bf16[1,4,10752]{2,1,0:T(4,128)(2,1)S(1)} %collective-permute-done.refs_1_, ...), custom_call_target="tpu_custom_call" | custom-call | flops 1073741824 | tf_op jit(solution)/shard_map/finish/pallas_call | solution.py:384
  (2 shorter events, 0.0 us)
Async XLA Ops:
  1.3 14.9 %copy-start = (f32[16,128]{1,0:T(8,128)S(1)}, f32[16,128]{1,0:T(8,128)}, u32[]{:S(2)}) copy-start(f32[16,128]{1,0:T(8,128)} %constant.10.clone.refs_4_.refs_11_) | copy-start | bytes 24580
  1.3 14.9 %copy-start.1 = (f32[16,128]{1,0:T(8,128)S(1)}, f32[16,128]{1,0:T(8,128)}, u32[]{:S(2)}) copy-start(f32[16,128]{1,0:T(8,128)} %constant.11.clone.refs_5_.refs_12_) | copy-start | bytes 24580
  6.8 9.3 %collective-permute-start.3 = (bf16[512,256]{1,0:T(8,128)(2,1)S(1)}, bf16[512,256]{1,0:T(8,128)(2,1)S(1)}, u32[]{:S(2)}, u32[]{:S(2)}) collective-permute-start(bf16[512,256]{1,0:T(8,128)(2,1)S(1)} %get-tuple-element.20.refs_0_.own_ref), channel_id=1, source_target_pairs={{0,2},{1,3},{2,0},{3,1},{4,6},{5,7},{6,4},{7,5},{8,10},{9,11},{10,... | collective-permute-start | bytes 786440 | tf_op jit(solution)/shard_map/ppermute | solution.py:443
  9.8 6.3 %collective-permute-start.5 = (bf16[512,256]{1,0:T(8,128)(2,1)S(1)}, bf16[512,256]{1,0:T(8,128)(2,1)S(1)}, u32[]{:S(2)}, u32[]{:S(2)}) collective-permute-start(bf16[512,256]{1,0:T(8,128)(2,1)S(1)} %get-tuple-element.20.refs_0_.own_ref), channel_id=1, source_target_pairs={{0,1},{1,0},{2,3},{3,2},{4,5},{5,4},{6,7},{7,6},{8,9},{9,8},{10,11... | collective-permute-start | bytes 786440 | tf_op jit(solution)/shard_map/ppermute | solution.py:374
  9.8 15.7 %collective-permute-start = (bf16[1,4,10752]{2,1,0:T(4,128)(2,1)S(1)}, bf16[1,4,10752]{2,1,0:T(4,128)(2,1)S(1)}, u32[]{:S(2)}, u32[]{:S(2)}) collective-permute-start(bf16[1,4,10752]{2,1,0:T(4,128)(2,1)S(1)} %get-tuple-element.19.refs_0_), channel_id=1, source_target_pairs={{0,8},{4,12},{8,0},{12,4},{1,9},{5,13},{9,1},{13,5},{2,10},{6,14},... | collective-permute-start | bytes 258056 | tf_op jit(solution)/shard_map/ppermute | solution.py:471
  12.4 13.3 %collective-permute-start.1 = (bf16[1,4,10752]{2,1,0:T(4,128)(2,1)S(1)}, bf16[1,4,10752]{2,1,0:T(4,128)(2,1)S(1)}, u32[]{:S(2)}, u32[]{:S(2)}) collective-permute-start(bf16[1,4,10752]{2,1,0:T(4,128)(2,1)S(1)} %get-tuple-element.19.refs_0_), channel_id=1, source_target_pairs={{0,12},{4,8},{8,4},{12,0},{1,13},{5,9},{9,5},{13,1},{2,14},{6,10},... | collective-permute-start | bytes 258056 | tf_op jit(solution)/shard_map/ppermute | solution.py:471
  13.8 12.0 %collective-permute-start.2 = (bf16[1,4,10752]{2,1,0:T(4,128)(2,1)S(1)}, bf16[1,4,10752]{2,1,0:T(4,128)(2,1)S(1)}, u32[]{:S(2)}, u32[]{:S(2)}) collective-permute-start(bf16[1,4,10752]{2,1,0:T(4,128)(2,1)S(1)} %get-tuple-element.19.refs_0_), channel_id=1, source_target_pairs={{0,4},{4,0},{8,12},{12,8},{1,5},{5,1},{9,13},{13,9},{2,6},{6,2},{1... | collective-permute-start | bytes 258056 | tf_op jit(solution)/shard_map/ppermute | solution.py:471
  16.1 1.7 %collective-permute-start.4 = (bf16[512,256]{1,0:T(8,128)(2,1)S(1)}, bf16[512,256]{1,0:T(8,128)(2,1)S(1)}, u32[]{:S(2)}, u32[]{:S(2)}) collective-permute-start(bf16[512,256]{1,0:T(8,128)(2,1)S(1)} %collective-permute-done.3.refs_0_), channel_id=1, source_target_pairs={{0,1},{1,0},{2,3},{3,2},{4,5},{5,4},{6,7},{7,6},{8,9},{9,8},{10,11... | collective-permute-start | bytes 786440 | tf_op jit(solution)/shard_map/ppermute | solution.py:374
  21.3 10.1 %collective-permute-start.6 = (bf16[1,4,10752]{2,1,0:T(4,128)(2,1)S(1)}, bf16[1,4,10752]{2,1,0:T(4,128)(2,1)S(1)}, u32[]{:S(2)}, u32[]{:S(2)}) collective-permute-start(bf16[1,4,10752]{2,1,0:T(4,128)(2,1)S(1)} %column_late.1.refs_4_), channel_id=1, source_target_pairs={{0,8},{4,12},{8,0},{12,4},{1,9},{5,13},{9,1},{13,5},{2,10},{6,14},... | collective-permute-start | bytes 258056 | tf_op jit(solution)/shard_map/ppermute | solution.py:471
  24.2 7.2 %collective-permute-start.7 = (bf16[1,4,10752]{2,1,0:T(4,128)(2,1)S(1)}, bf16[1,4,10752]{2,1,0:T(4,128)(2,1)S(1)}, u32[]{:S(2)}, u32[]{:S(2)}) collective-permute-start(bf16[1,4,10752]{2,1,0:T(4,128)(2,1)S(1)} %column_late.1.refs_4_), channel_id=1, source_target_pairs={{0,12},{4,8},{8,4},{12,0},{1,13},{5,9},{9,5},{13,1},{2,14},{6,10},... | collective-permute-start | bytes 258056 | tf_op jit(solution)/shard_map/ppermute | solution.py:471
  25.5 6.9 %collective-permute-start.8 = (bf16[1,4,10752]{2,1,0:T(4,128)(2,1)S(1)}, bf16[1,4,10752]{2,1,0:T(4,128)(2,1)S(1)}, u32[]{:S(2)}, u32[]{:S(2)}) collective-permute-start(bf16[1,4,10752]{2,1,0:T(4,128)(2,1)S(1)} %column_late.1.refs_4_), channel_id=1, source_target_pairs={{0,4},{4,0},{8,12},{12,8},{1,5},{5,1},{9,13},{13,9},{2,6},{6,2},{1... | collective-permute-start | bytes 258056 | tf_op jit(solution)/shard_map/ppermute | solution.py:471

commit v4 on v3

--- a/solution.py
+++ b/solution.py
@@ -17,6 +17,8 @@
 VMEM_LIMIT = 32 * 1024 * 1024
 ROW_VMEM_LIMIT = 62 * 1024 * 1024
 WORK_UNIT = 1 << 30
+FIRST_WORK = 3
+MORE_WORK = 3
 F32 = jnp.float32
 BF16 = jnp.bfloat16
 
@@ -283,11 +285,9 @@
     return keys
 
 
-def early_kernel(blocks, rows, cols, *refs):
-    h_refs = refs[: len(blocks)]
-    w_qkv_ref, w_ao_ref, cos_ref, sin_ref = refs[len(blocks) : len(blocks) + 4]
-    q_ref, left_ref, right_ref, den_ref, w_kv_ref, w_o_ref = refs[len(blocks) + 4 :]
-    width = h_refs[0].shape[-1]
+def first_kernel(rows, cols, own_ref, *refs):
+    w_qkv_ref, w_ao_ref, cos_ref, sin_ref, q_ref, left_ref, right_ref, den_ref, w_kv_ref, w_o_ref = refs
+    width = own_ref.shape[-1]
     head = width // HEADS
     half = head // 2
     wide = width // 2
@@ -300,14 +300,27 @@
     w_o_ref[...] = lax.dot_general(
         pick, w_ao_ref[...], (((0,), (0,)), ((), ())), preferred_element_type=F32
     ).astype(BF16)
-    part = dot(rms_round(h_refs[0][...]), w_q)
+    part = dot(rms_round(own_ref[...]), w_q)
     left, right = turn_rows(rows, cols, wide, 0, part, 1.0 / math.sqrt(head), cos_ref, sin_ref)
     q_left, q_right = jnp.stack(left), jnp.stack(right)
     q_ref[:, :, :wide] = q_left
     q_ref[:, :, wide:] = q_right
-    keys = all_keys(rows, cols, half, blocks, h_refs, w_k, w_v, cos_ref, sin_ref)
+    keys = all_keys(rows, cols, half, [0], [own_ref], w_k, w_v, cos_ref, sin_ref)
     totals = (jnp.zeros((rows, cols, wide), F32),) * 3
     left_ref[...], right_ref[...], den_ref[...] = mix_rows(rows, cols, half, q_left, q_right, keys, totals)
+
+
+def more_kernel(blocks, rows, cols, *refs):
+    h_refs = refs[: len(blocks)]
+    q_ref, left_in, right_in, den_in, w_kv_ref, cos_ref, sin_ref, left_ref, right_ref, den_ref = refs[len(blocks) :]
+    width = q_ref.shape[-1]
+    half = width // HEADS // 2
+    wide = width // 2
+    keys = all_keys(rows, cols, half, blocks, h_refs, w_kv_ref[:, :width], w_kv_ref[:, width:], cos_ref, sin_ref)
+    totals = (left_in[...], right_in[...], den_in[...])
+    left_ref[...], right_ref[...], den_ref[...] = mix_rows(
+        rows, cols, half, q_ref[:, :, :wide], q_ref[:, :, wide:], keys, totals
+    )
 
 
 def late_kernel(blocks, rows, cols, chan, own_ref, *refs):
@@ -441,25 +454,33 @@
         top = n_row // 2
         early = cube(hidden, "row", n_row, top)
         across = lax.ppermute(hidden, "row", [(i, i ^ top) for i in range(n_row)])
-        early_ids, late_ids = list(range(top)), list(range(top, n_row))
         down = rotary_angles(n_row * rows, half, width // 2)
         tables = [jnp.asarray(np.cos(down), F32), jnp.asarray(np.sin(down), F32)]
         piece = like((rows, cols, width // 2), F32)
-        *sums, w_kv, w_o = kernel_call(
-            functools.partial(early_kernel, early_ids, rows, cols), "column_early",
-            (*early, w_qkv1, w_ao1, *tables),
-            [VMEM_SPEC] * (top + 4),
+        query, *sums, w_kv, w_o = kernel_call(
+            functools.partial(first_kernel, rows, cols), "column_first",
+            (hidden, w_qkv1, w_ao1, *tables),
+            [VMEM_SPEC] * 5,
             [
                 like((rows, cols, width), BF16), piece, piece, piece,
                 like((width, 2 * width), BF16), like((width, width), BF16),
             ],
-            3 * WORK_UNIT,
+            FIRST_WORK * WORK_UNIT,
         )
-        late = cube(across, "row", n_row, top)
+        middle = [*early[1:], across]
+        sums = kernel_call(
+            functools.partial(more_kernel, list(range(1, top + 1)), rows, cols), "column_early",
+            (*middle, query, *sums, w_kv, *tables),
+            [VMEM_SPEC] * (len(middle) + 7),
+            [piece, piece, piece],
+            MORE_WORK * WORK_UNIT,
+        )
+        late = cube(across, "row", n_row, top)[1:]
+        late_ids = list(range(top + 1, n_row))
         own_pred = kernel_call(
             functools.partial(late_kernel, late_ids, rows, cols, chan), "column_late",
-            (hidden, *late, *sums, w_kv, w_o, w_up1, w_down1, w_out1, *tables),
-            [VMEM_SPEC] * (top + 12),
+            (hidden, *late, query, *sums, w_kv, w_o, w_up1, w_down1, w_out1, *tables),
+            [VMEM_SPEC] * (len(late) + 12),
             like((1, rows, flat), BF16),
             5 * WORK_UNIT,
             [pltpu.VMEM((rows * cols, LANES), F32)],

time: 34 us -> 33 us (0.971)
  waiting for transfers between devices: 8.83 us -> 7.71 us
    ppermute x1, waiting for transfers between devices: 2.14 us -> 0.99 us  [per_device(): across = lax.ppermute(hidden, 'row', [(i, i ^ top) for i in range(n_row)])]
    pallas_call x4 -> x5, Pallas kernels: 12 us -> 12.1 us  [kernel_call(): pl.pallas_call(body, out_shape=outs, in_specs=specs, out_specs=out_specs,...]
  transfers between devices with their start and end apart: 9 -> 9, of which waited for: 3 -> 4; matrix products, arithmetic and copies ran while one was open for 0% -> 0% of each run, Pallas kernels for 15% -> 16%
where the time goes in v4:
time: 33 us; the launch traced here: 32.8 us
  Pallas kernels  12.1 us (37%)
  starting transfers between devices  11.7 us (35%)
  waiting for transfers between devices  7.71 us (23%)
  between operations  1.33 us (4%)
    pallas_call x5, Pallas kernels, kernel_call(): pl.pallas_call(body, out_shape=outs, in_specs=specs, out_specs=out_specs,...  12.1 us
    ppermute x6, starting transfers between devices, spread(): lax.ppermute(value, 'dom', [(i, i ^ k) for i in range(n_dom)])  8.65 us
    ppermute x6, waiting for transfers between devices, spread(): lax.ppermute(value, 'dom', [(i, i ^ k) for i in range(n_dom)])  6.66 us
    ppermute x1, starting transfers between devices, per_device(): across = lax.ppermute(hidden, 'row', [(i, i ^ top) for i in range(n_row)])  3.01 us
    ppermute x1, waiting for transfers between devices, per_device(): across = lax.ppermute(hidden, 'row', [(i, i ^ top) for i in range(n_row)])  0.99 us
  transfers between devices with their start and end apart: 9, of which 4 were waited for; matrix products, arithmetic and copies ran while one was open for 0% of the time, Pallas kernels for 16%

profile of v4, /device:TPU:0, one launch (start us, length us, event | category | flops | bytes accessed | tf_op | source)
XLA Modules:
  0.0 32.8 jit_solution(12934776470226375221)
XLA Ops:
  1.3 0.0 copy-start
  1.3 0.0 copy-start.1
  1.3 5.5 %row_block.1 = (bf16[512,256]{1,0:T(8,128)(2,1)S(1)}, bf16[1,4,10752]{2,1,0:T(4,128)(2,1)S(1)}, f32[2,128]{1,0:T(2,128)S(1)}, s32[1]{0:T(128)}, bf16[256,768]{1,...) custom-call(s32[1]{0:T(128)S(6)} %copy.17.time_ref, ...), custom_call_target="tpu_custom_call" | custom-call | flops 5368709120 | tf_op jit(solution)/shard_map/row_block/pallas_call | solution.py:397
  6.8 3.0 %collective-permute-start.3 = (bf16[512,256]{1,0:T(8,128)(2,1)S(1)}, bf16[512,256]{1,0:T(8,128)(2,1)S(1)}, u32[]{:S(2)}, u32[]{:S(2)}) collective-permute-start(bf16[512,256]{1,0:T(8,128)(2,1)S(1)} %get-tuple-element.23.own_ref), channel_id=1, source_target_pairs={{0,2},{1,3},{2,0},{3,1},{4,6},{5,7},{6,4},{7,5},{8,10},{9,11},{10,... | collective-permute-start | bytes 786440 | tf_op jit(solution)/shard_map/ppermute | solution.py:456
  9.8 0.0 collective-permute-start.5
  9.8 2.6 %collective-permute-start = (bf16[1,4,10752]{2,1,0:T(4,128)(2,1)S(1)}, bf16[1,4,10752]{2,1,0:T(4,128)(2,1)S(1)}, u32[]{:S(2)}, u32[]{:S(2)}) collective-permute-start(bf16[1,4,10752]{2,1,0:T(4,128)(2,1)S(1)} %get-tuple-element.22.refs_0_), channel_id=1, source_target_pairs={{0,8},{4,12},{8,0},{12,4},{1,9},{5,13},{9,1},{13,5},{2,10},{6,14},... | collective-permute-start | bytes 258056 | tf_op jit(solution)/shard_map/ppermute | solution.py:492
  12.4 1.3 %collective-permute-start.1 = (bf16[1,4,10752]{2,1,0:T(4,128)(2,1)S(1)}, bf16[1,4,10752]{2,1,0:T(4,128)(2,1)S(1)}, u32[]{:S(2)}, u32[]{:S(2)}) collective-permute-start(bf16[1,4,10752]{2,1,0:T(4,128)(2,1)S(1)} %get-tuple-element.22.refs_0_), channel_id=1, source_target_pairs={{0,12},{4,8},{8,4},{12,0},{1,13},{5,9},{9,5},{13,1},{2,14},{6,10},... | collective-permute-start | bytes 258056 | tf_op jit(solution)/shard_map/ppermute | solution.py:492
  13.8 0.2 collective-permute-start.2
  14.0 1.1 %column_first.1 = (bf16[4,128,256]{2,1,0:T(8,128)(2,1)S(1)}, f32[4,128,128]{2,1,0:T(8,128)S(1)}, f32[4,128,128]{2,1,0:T(8,128)S(1)}, f32[4,128,128]{2,1,0:T(8,12...) custom-call(bf16[512,256]{1,0:T(8,128)(2,1)S(1)} %get-tuple-element.23.own_ref, ...), custom_call_target="tpu_custom_call" | custom-call | flops 3221225472 | tf_op jit(solution)/shard_map/column_first/pallas_call | solution.py:397
  15.1 1.0 %collective-permute-done.3.refs_1_ = bf16[512,256]{1,0:T(8,128)(2,1)S(1)} collective-permute-done((bf16[512,256]{1,0:T(8,128)(2,1)S(1)}, bf16[512,256]{1,0:T(8,128)(2,1)S(1)}, u32[]{:S(2)}, u32[]{:S(2)}) %collective-permute-start.3) | collective-permute-done | bytes 262176 | tf_op jit(solution)/shard_map/ppermute | solution.py:456
  16.1 0.0 collective-permute-start.4
  16.1 0.0 collective-permute-done.5.refs_0_
  16.1 1.5 %column_early.1 = (f32[4,128,128]{2,1,0:T(8,128)S(1)}, f32[4,128,128]{2,1,0:T(8,128)S(1)}, f32[4,128,128]{2,1,0:T(8,128)S(1)}) custom-call(bf16[512,256]{1,0:T(8,128)(2,1)S(1)} %collective-permute-done.5.refs_0_, bf16[512,256]{1,0:T(8,128)(2,1)S(1)} %collective-permute-done.3.refs_1_, bf16[4,128,256]{2,1,0:T(8,128)(2,1)S(1)} %get-tuple-element.26.refs_2_.refs_1_, ...), custom_call_target="tpu_custom_call" | custom-call | flops 3221225472 | tf_op jit(solution)/shard_map/column_early/pallas_call | solution.py:397
  17.6 0.1 collective-permute-done.4.refs_0_
  17.7 2.7 %column_late.1.refs_4_ = bf16[1,4,10752]{2,1,0:T(4,128)(2,1)S(1)} custom-call(bf16[512,256]{1,0:T(8,128)(2,1)S(1)} %get-tuple-element.23.own_ref, bf16[512,256]{1,0:T(8,128)(2,1)S(1)} %collective-permute-done.4.refs_0_, bf16[4,128,256]{2,1,0:T(8,128)(2,1)S(1)} %get-tuple-element.26.refs_2_.refs_1_, f32[4,128,128]{2,1,0:T(8,128)S(1)} %get-tuple-element.31.refs_2_, ...), custom_call_target="tpu_custom_call" | custom-call | flops 5368709120 | tf_op jit(solution)/shard_map/column_late/pallas_call | solution.py:397
  20.4 2.9 %collective-permute-start.6 = (bf16[1,4,10752]{2,1,0:T(4,128)(2,1)S(1)}, bf16[1,4,10752]{2,1,0:T(4,128)(2,1)S(1)}, u32[]{:S(2)}, u32[]{:S(2)}) collective-permute-start(bf16[1,4,10752]{2,1,0:T(4,128)(2,1)S(1)} %column_late.1.refs_4_), channel_id=1, source_target_pairs={{0,8},{4,12},{8,0},{12,4},{1,9},{5,13},{9,1},{13,5},{2,10},{6,14},... | collective-permute-start | bytes 258056 | tf_op jit(solution)/shard_map/ppermute | solution.py:492
  23.3 1.3 %collective-permute-start.7 = (bf16[1,4,10752]{2,1,0:T(4,128)(2,1)S(1)}, bf16[1,4,10752]{2,1,0:T(4,128)(2,1)S(1)}, u32[]{:S(2)}, u32[]{:S(2)}) collective-permute-start(bf16[1,4,10752]{2,1,0:T(4,128)(2,1)S(1)} %column_late.1.refs_4_), channel_id=1, source_target_pairs={{0,12},{4,8},{8,4},{12,0},{1,13},{5,9},{9,5},{13,1},{2,14},{6,10},... | collective-permute-start | bytes 258056 | tf_op jit(solution)/shard_map/ppermute | solution.py:492
  24.6 0.0 collective-permute-done.refs_1_
  24.6 0.2 collective-permute-start.8
  24.9 0.0 collective-permute-done.1.refs_2_
  24.9 0.0 collective-permute-done.2.refs_3_
  24.9 5.6 %collective-permute-done.6.refs_5_ = bf16[1,4,10752]{2,1,0:T(4,128)(2,1)S(1)} collective-permute-done((bf16[1,4,10752]{2,1,0:T(4,128)(2,1)S(1)}, bf16[1,4,10752]{2,1,0:T(4,128)(2,1)S(1)}, u32[]{:S(2)}, u32[]{:S(2)}) %collective-permute-start.6) | collective-permute-done | bytes 86048 | tf_op jit(solution)/shard_map/ppermute | solution.py:492
  30.5 1.0 %collective-permute-done.8.refs_7_ = bf16[1,4,10752]{2,1,0:T(4,128)(2,1)S(1)} collective-permute-done((bf16[1,4,10752]{2,1,0:T(4,128)(2,1)S(1)}, bf16[1,4,10752]{2,1,0:T(4,128)(2,1)S(1)}, u32[]{:S(2)}, u32[]{:S(2)}) %collective-permute-start.8) | collective-permute-done | bytes 86048 | tf_op jit(solution)/shard_map/ppermute | solution.py:492
  31.5 1.3 %finish.1 = (bf16[1,4,10752]{2,1,0:T(4,128)(2,1)}, bf16[1,4,10752]{2,1,0:T(4,128)(2,1)}) custom-call(s32[1]{0:T(128)} %get-tuple-element.20.pick_ref, f32[2,128]{1,0:T(2,128)S(1)} %get-tuple-element.21.coef_ref, bf16[1,4,10752]{2,1,0:T(4,128)(2,1)S(1)} %get-tuple-element.22.refs_0_, bf16[1,4,10752]{2,1,0:T(4,128)(2,1)S(1)} %collective-permute-done.refs_1_, ...), custom_call_target="tpu_custom_call" | custom-call | flops 1073741824 | tf_op jit(solution)/shard_map/finish/pallas_call | solution.py:397
  (3 shorter events, 0.0 us)
Async XLA Ops:
  1.3 12.7 %copy-start = (f32[16,128]{1,0:T(8,128)S(1)}, f32[16,128]{1,0:T(8,128)}, u32[]{:S(2)}) copy-start(f32[16,128]{1,0:T(8,128)} %constant.10.clone.refs_2_.refs_7_.refs_10_) | copy-start | bytes 24580
  1.3 12.7 %copy-start.1 = (f32[16,128]{1,0:T(8,128)S(1)}, f32[16,128]{1,0:T(8,128)}, u32[]{:S(2)}) copy-start(f32[16,128]{1,0:T(8,128)} %constant.11.clone.refs_3_.refs_8_.refs_11_) | copy-start | bytes 24580
  6.8 9.3 %collective-permute-start.3 = (bf16[512,256]{1,0:T(8,128)(2,1)S(1)}, bf16[512,256]{1,0:T(8,128)(2,1)S(1)}, u32[]{:S(2)}, u32[]{:S(2)}) collective-permute-start(bf16[512,256]{1,0:T(8,128)(2,1)S(1)} %get-tuple-element.23.own_ref), channel_id=1, source_target_pairs={{0,2},{1,3},{2,0},{3,1},{4,6},{5,7},{6,4},{7,5},{8,10},{9,11},{10,... | collective-permute-start | bytes 786440 | tf_op jit(solution)/shard_map/ppermute | solution.py:456
  9.8 6.3 %collective-permute-start.5 = (bf16[512,256]{1,0:T(8,128)(2,1)S(1)}, bf16[512,256]{1,0:T(8,128)(2,1)S(1)}, u32[]{:S(2)}, u32[]{:S(2)}) collective-permute-start(bf16[512,256]{1,0:T(8,128)(2,1)S(1)} %get-tuple-element.23.own_ref), channel_id=1, source_target_pairs={{0,1},{1,0},{2,3},{3,2},{4,5},{5,4},{6,7},{7,6},{8,9},{9,8},{10,11... | collective-permute-start | bytes 786440 | tf_op jit(solution)/shard_map/ppermute | solution.py:387
  9.8 14.8 %collective-permute-start = (bf16[1,4,10752]{2,1,0:T(4,128)(2,1)S(1)}, bf16[1,4,10752]{2,1,0:T(4,128)(2,1)S(1)}, u32[]{:S(2)}, u32[]{:S(2)}) collective-permute-start(bf16[1,4,10752]{2,1,0:T(4,128)(2,1)S(1)} %get-tuple-element.22.refs_0_), channel_id=1, source_target_pairs={{0,8},{4,12},{8,0},{12,4},{1,9},{5,13},{9,1},{13,5},{2,10},{6,14},... | collective-permute-start | bytes 258056 | tf_op jit(solution)/shard_map/ppermute | solution.py:492
  12.4 12.4 %collective-permute-start.1 = (bf16[1,4,10752]{2,1,0:T(4,128)(2,1)S(1)}, bf16[1,4,10752]{2,1,0:T(4,128)(2,1)S(1)}, u32[]{:S(2)}, u32[]{:S(2)}) collective-permute-start(bf16[1,4,10752]{2,1,0:T(4,128)(2,1)S(1)} %get-tuple-element.22.refs_0_), channel_id=1, source_target_pairs={{0,12},{4,8},{8,4},{12,0},{1,13},{5,9},{9,5},{13,1},{2,14},{6,10},... | collective-permute-start | bytes 258056 | tf_op jit(solution)/shard_map/ppermute | solution.py:492
  13.8 11.1 %collective-permute-start.2 = (bf16[1,4,10752]{2,1,0:T(4,128)(2,1)S(1)}, bf16[1,4,10752]{2,1,0:T(4,128)(2,1)S(1)}, u32[]{:S(2)}, u32[]{:S(2)}) collective-permute-start(bf16[1,4,10752]{2,1,0:T(4,128)(2,1)S(1)} %get-tuple-element.22.refs_0_), channel_id=1, source_target_pairs={{0,4},{4,0},{8,12},{12,8},{1,5},{5,1},{9,13},{13,9},{2,6},{6,2},{1... | collective-permute-start | bytes 258056 | tf_op jit(solution)/shard_map/ppermute | solution.py:492
  16.1 1.5 %collective-permute-start.4 = (bf16[512,256]{1,0:T(8,128)(2,1)S(1)}, bf16[512,256]{1,0:T(8,128)(2,1)S(1)}, u32[]{:S(2)}, u32[]{:S(2)}) collective-permute-start(bf16[512,256]{1,0:T(8,128)(2,1)S(1)} %collective-permute-done.3.refs_1_), channel_id=1, source_target_pairs={{0,1},{1,0},{2,3},{3,2},{4,5},{5,4},{6,7},{7,6},{8,9},{9,8},{10,11... | collective-permute-start | bytes 786440 | tf_op jit(solution)/shard_map/ppermute | solution.py:387
  20.4 10.1 %collective-permute-start.6 = (bf16[1,4,10752]{2,1,0:T(4,128)(2,1)S(1)}, bf16[1,4,10752]{2,1,0:T(4,128)(2,1)S(1)}, u32[]{:S(2)}, u32[]{:S(2)}) collective-permute-start(bf16[1,4,10752]{2,1,0:T(4,128)(2,1)S(1)} %column_late.1.refs_4_), channel_id=1, source_target_pairs={{0,8},{4,12},{8,0},{12,4},{1,9},{5,13},{9,1},{13,5},{2,10},{6,14},... | collective-permute-start | bytes 258056 | tf_op jit(solution)/shard_map/ppermute | solution.py:492
  23.3 7.2 %collective-permute-start.7 = (bf16[1,4,10752]{2,1,0:T(4,128)(2,1)S(1)}, bf16[1,4,10752]{2,1,0:T(4,128)(2,1)S(1)}, u32[]{:S(2)}, u32[]{:S(2)}) collective-permute-start(bf16[1,4,10752]{2,1,0:T(4,128)(2,1)S(1)} %column_late.1.refs_4_), channel_id=1, source_target_pairs={{0,12},{4,8},{8,4},{12,0},{1,13},{5,9},{9,5},{13,1},{2,14},{6,10},... | collective-permute-start | bytes 258056 | tf_op jit(solution)/shard_map/ppermute | solution.py:492
  24.6 6.9 %collective-permute-start.8 = (bf16[1,4,10752]{2,1,0:T(4,128)(2,1)S(1)}, bf16[1,4,10752]{2,1,0:T(4,128)(2,1)S(1)}, u32[]{:S(2)}, u32[]{:S(2)}) collective-permute-start(bf16[1,4,10752]{2,1,0:T(4,128)(2,1)S(1)} %column_late.1.refs_4_), channel_id=1, source_target_pairs={{0,4},{4,0},{8,12},{12,8},{1,5},{5,1},{9,13},{13,9},{2,6},{6,2},{1... | collective-permute-start | bytes 258056 | tf_op jit(solution)/shard_map/ppermute | solution.py:492

commit v5 on v4

--- a/solution.py
+++ b/solution.py
@@ -137,9 +137,9 @@
 
 
 def row_kernel(
-    rows, cols, chan,
+    rows, cols, chan, small,
     time_ref, anc_ref, state_ref, prev_ref, w_time_ref, w_in_ref, w_qkv_ref, cos_ref, sin_ref, w_ao_ref, w_up_ref, w_down_ref, w_out_ref,
-    out_ref, state_scr, coef_ref, pick_ref, next_qkv_ref, next_ao_ref, next_up_ref, next_down_ref, next_out_ref,
+    out_ref, state_scr, coef_ref, pick_ref, need_ref, next_qkv_ref, next_ao_ref, next_up_ref, next_down_ref, next_out_ref,
     anc_scr, prev_scr, w_time_scr, w_in_scr, w_qkv_scr, cos_scr, sin_scr, w_ao_scr, w_up_scr, w_down_scr,
     flat_scr, tok_scr, sems,
 ):
@@ -235,6 +235,11 @@
     for copy in copies[11:] + copies[:1]:
         copy.wait()
     pick_ref[0] = anc_scr[lax.axis_index("dom")]
+    need = jnp.int32(0)
+    if small:
+        for j in range(anc_scr.shape[0]):
+            need = lax.bitwise_or(need, lax.shift_left(jnp.int32(1), lax.bitwise_xor(anc_scr[j], jnp.int32(j))))
+    need_ref[0] = lax.shift_right_logical(need, jnp.int32(1))
 
 
 def project_keys(rows, cols, half, block, h_ref, w_k, w_v, cos_ref, sin_ref):
@@ -427,15 +432,16 @@
         vmem = lambda arr: pltpu.VMEM(arr.shape, arr.dtype)
         block_vmem = lambda arr: pltpu.VMEM(arr.shape[1:], arr.dtype)
         my_dom = lax.axis_index("dom").astype(jnp.int32)
+        small = n_dom in (2, 4)
         inputs = (
             timestep, ancestors, state, prev_pred, w_time, w_in, w_qkv, *tables, w_attn_out, w_up, w_down, w_out.T,
         )
-        hidden, state_out, coefs, pick, *weights = kernel_call(
-            functools.partial(row_kernel, rows, cols, chan), "row_block",
+        hidden, state_out, coefs, pick, need, *weights = kernel_call(
+            functools.partial(row_kernel, rows, cols, chan, small), "row_block",
             (timestep, *[pltpu.with_memory_space_constraint(x, pltpu.HBM) for x in inputs[1:]]),
             [SMEM_SPEC] + [HBM_SPEC] * (len(inputs) - 1),
             [
-                like((rows * cols, width), BF16), like_of(state), like((2, LANES), F32), like((1,), jnp.int32),
+                like((rows * cols, width), BF16), like_of(state), like((2, LANES), F32), like((1,), jnp.int32), like((1,), jnp.int32),
                 block_of(w_qkv), block_of(w_attn_out), block_of(w_up), block_of(w_down), like_of(w_out.T),
             ],
             5 * WORK_UNIT,
@@ -447,7 +453,7 @@
                 pltpu.VMEM((2 * rows * cols, LANES), F32),
                 pltpu.SemaphoreType.DMA((16,)),
             ],
-            [VMEM_SPEC] * 3 + [SMEM_SPEC] + [VMEM_SPEC] * 5,
+            [VMEM_SPEC] * 3 + [SMEM_SPEC] * 2 + [VMEM_SPEC] * 5,
         )
         w_qkv1, w_ao1, w_up1, w_down1, w_out1 = weights
 
@@ -486,30 +492,40 @@
             [pltpu.VMEM((rows * cols, LANES), F32)],
         )
 
-        if n_dom & (n_dom - 1) == 0 and n_dom <= 8:
-
-            def spread(value):
-                got = [lax.ppermute(value, "dom", [(i, i ^ k) for i in range(n_dom)]) for k in range(n_dom - 1, 0, -1)]
-                return [value] + got[::-1]
-        else:
-
-            def spread(value):
-                every = lax.all_gather(value, "dom")
-                return [lax.dynamic_index_in_dim(every, ancestors[my_dom], 0, keepdims=False)]
-
-        states, preds = spread(state_out), spread(own_pred)
         shape = like(state.shape, BF16)
-        turn = list(range(0, len(preds), 2)) + list(range(len(preds) - 1, 0, -2))
-        states, preds = [[x[i] for i in turn] for x in (states, preds)]
-        return kernel_call(
-            functools.partial(finish_kernel, turn), "finish",
-            (pick, coefs, *states, *preds),
-            [SMEM_SPEC] + [VMEM_SPEC] * (1 + 2 * len(preds)),
-            (shape, shape),
-            WORK_UNIT,
-            [pltpu.VMEM(state.shape, BF16), pltpu.SemaphoreType.DMA((2,))],
-            (HBM_SPEC, HBM_SPEC),
-        )
+
+        def finish(turn, states, preds, coefs, pick):
+            return kernel_call(
+                functools.partial(finish_kernel, turn), "finish",
+                (pick, coefs, *states, *preds),
+                [SMEM_SPEC] + [VMEM_SPEC] * (1 + 2 * len(preds)),
+                (shape, shape),
+                WORK_UNIT,
+                [pltpu.VMEM(state.shape, BF16), pltpu.SemaphoreType.DMA((2,))],
+                (HBM_SPEC, HBM_SPEC),
+            )
+
+        if not small:
+            every = [
+                lax.dynamic_index_in_dim(lax.all_gather(x, "dom"), ancestors[my_dom], 0, keepdims=False)
+                for x in (state_out, own_pred)
+            ]
+            return finish([0], every[:1], every[1:], coefs, pick)
+
+        def swap(value, k):
+            return lax.ppermute(value, "dom", [(i, i ^ k) for i in range(n_dom)])
+
+        def gather(turn, states, own_pred, coefs, pick):
+            preds = [own_pred] + [swap(own_pred, k) for k in turn]
+            return finish([0, *turn], [states[0]] + [states[k] for k in turn], preds, coefs, pick)
+
+        turn = list(range(2, n_dom)) + [1]
+        states = [state_out] + [swap(state_out, k) for k in turn]
+        states = {0: states[0], **dict(zip(turn, states[1:]))}
+        branches = [
+            functools.partial(gather, [k for k in turn if (code >> k) & 1]) for code in range(0, 1 << n_dom, 2)
+        ]
+        return lax.switch(need[0], branches, states, own_pred, coefs, pick)
 
     return per_device
 

time: 33 us -> 29.9 us (0.906)
  the two profiles are of different devices: /device:TPU:0 before, /device:TPU:4 now
where the time goes in v5:
time: 29.9 us; the launch traced here: 29.7 us
  Pallas kernels  12.4 us (41%)
  starting transfers between devices  9.36 us (31%)
  waiting for transfers between devices  5.95 us (20%)
  between operations  2.01 us (7%)
    pallas_call x5, Pallas kernels, kernel_call(): pl.pallas_call(body, out_shape=outs, in_specs=specs, out_specs=out_specs,...  12.4 us
    ppermute x5, starting transfers between devices, swap(): return lax.ppermute(value, 'dom', [(i, i ^ k) for i in range(n_dom)])  7.8 us
    ppermute x5, waiting for transfers between devices, swap(): return lax.ppermute(value, 'dom', [(i, i ^ k) for i in range(n_dom)])  5.6 us
    ppermute x1, starting transfers between devices, per_device(): across = lax.ppermute(hidden, 'row', [(i, i ^ top) for i in range(n_row)])  1.55 us
  transfers between devices with their start and end apart: 8, of which 4 were waited for; matrix products, arithmetic and copies ran while one was open for 0% of the time, Pallas kernels for 18%

profile of v5, /device:TPU:4, one launch (start us, length us, event | category | flops | bytes accessed | tf_op | source)
XLA Modules:
  0.0 29.7 jit_solution(4765357912332102128)
XLA Ops:
  1.3 0.0 copy-start.1
  1.3 5.5 %row_block.1 = (bf16[512,256]{1,0:T(8,128)(2,1)S(1)}, bf16[1,4,10752]{2,1,0:T(4,128)(2,1)S(1)}, f32[2,128]{1,0:T(2,128)S(1)}, s32[1]{0:T(128)}, s32[1]{0:T(128)}...) custom-call(s32[1]{0:T(128)S(6)} %copy.49.time_ref, ...), custom_call_target="tpu_custom_call" | custom-call | flops 5368709120 | tf_op jit(solution)/shard_map/row_block/pallas_call | solution.py:402
  6.8 0.0 copy-start
  6.8 1.6 %collective-permute-start.12 = (bf16[512,256]{1,0:T(8,128)(2,1)S(1)}, bf16[512,256]{1,0:T(8,128)(2,1)S(1)}, u32[]{:S(2)}, u32[]{:S(2)}) collective-permute-start(bf16[512,256]{1,0:T(8,128)(2,1)S(1)} %get-tuple-element.157.own_ref), channel_id=1, source_target_pairs={{0,2},{1,3},{2,0},{3,1},{4,6},{5,7},{6,4},{7,5},{8,10},{9,11},{10,... | collective-permute-start | bytes 786440 | tf_op jit(solution)/shard_map/ppermute | solution.py:462
  8.4 0.0 collective-permute-start.14
  8.4 1.6 %collective-permute-start.15 = (bf16[1,4,10752]{2,1,0:T(4,128)(2,1)S(1)}, bf16[1,4,10752]{2,1,0:T(4,128)(2,1)S(1)}, u32[]{:S(2)}, u32[]{:S(2)}) collective-permute-start(bf16[1,4,10752]{2,1,0:T(4,128)(2,1)S(1)} %get-tuple-element.156), channel_id=1, source_target_pairs={{0,4},{4,0},{8,12},{12,8},{1,5},{5,1},{9,13},{13,9},{2,6},{6,2},{1... | collective-permute-start | bytes 258056 | tf_op jit(solution)/shard_map/ppermute | solution.py:516
  10.0 2.6 %collective-permute-start.16 = (bf16[1,4,10752]{2,1,0:T(4,128)(2,1)S(1)}, bf16[1,4,10752]{2,1,0:T(4,128)(2,1)S(1)}, u32[]{:S(2)}, u32[]{:S(2)}) collective-permute-start(bf16[1,4,10752]{2,1,0:T(4,128)(2,1)S(1)} %get-tuple-element.156), channel_id=1, source_target_pairs={{0,8},{4,12},{8,0},{12,4},{1,9},{5,13},{9,1},{13,5},{2,10},{6,14},... | collective-permute-start | bytes 258056 | tf_op jit(solution)/shard_map/ppermute | solution.py:516
  12.6 0.2 collective-permute-start.17
  13.5 1.1 %column_first.1 = (bf16[4,128,256]{2,1,0:T(8,128)(2,1)S(1)}, f32[4,128,128]{2,1,0:T(8,128)S(1)}, f32[4,128,128]{2,1,0:T(8,128)S(1)}, f32[4,128,128]{2,1,0:T(8,12...) custom-call(bf16[512,256]{1,0:T(8,128)(2,1)S(1)} %get-tuple-element.157.own_ref, ...), custom_call_target="tpu_custom_call" | custom-call | flops 3221225472 | tf_op jit(solution)/shard_map/column_first/pallas_call | solution.py:402
  14.6 0.3 %collective-permute-done.12.refs_1_ = bf16[512,256]{1,0:T(8,128)(2,1)S(1)} collective-permute-done((bf16[512,256]{1,0:T(8,128)(2,1)S(1)}, bf16[512,256]{1,0:T(8,128)(2,1)S(1)}, u32[]{:S(2)}, u32[]{:S(2)}) %collective-permute-start.12) | collective-permute-done | bytes 262176 | tf_op jit(solution)/shard_map/ppermute | solution.py:462
  14.9 0.0 collective-permute-start.13
  15.0 0.0 collective-permute-done.14.refs_0_
  15.0 1.5 %column_early.1 = (f32[4,128,128]{2,1,0:T(8,128)S(1)}, f32[4,128,128]{2,1,0:T(8,128)S(1)}, f32[4,128,128]{2,1,0:T(8,128)S(1)}) custom-call(bf16[512,256]{1,0:T(8,128)(2,1)S(1)} %collective-permute-done.14.refs_0_, bf16[512,256]{1,0:T(8,128)(2,1)S(1)} %collective-permute-done.12.refs_1_, bf16[4,128,256]{2,1,0:T(8,128)(2,1)S(1)} %get-tuple-element.160.refs_2_.refs_1_, ...), custom_call_target="tpu_custom_call" | custom-call | flops 3221225472 | tf_op jit(solution)/shard_map/column_early/pallas_call | solution.py:402
  16.5 0.0 collective-permute-done.13.refs_0_
  16.5 2.7 %column_late.1 = bf16[1,4,10752]{2,1,0:T(4,128)(2,1)S(1)} custom-call(bf16[512,256]{1,0:T(8,128)(2,1)S(1)} %get-tuple-element.157.own_ref, bf16[512,256]{1,0:T(8,128)(2,1)S(1)} %collective-permute-done.13.refs_0_, bf16[4,128,256]{2,1,0:T(8,128)(2,1)S(1)} %get-tuple-element.160.refs_2_.refs_1_, f32[4,128,128]{2,1,0:T(8,128)S(1)} %get-tuple-element.165.refs_2_, ...), custom_call_target="tpu_custom_call" | custom-call | flops 5368709120 | tf_op jit(solution)/shard_map/column_late/pallas_call | solution.py:402
  19.3 0.6 %collective-permute-done.16 = bf16[1,4,10752]{2,1,0:T(4,128)(2,1)S(1)} collective-permute-done((bf16[1,4,10752]{2,1,0:T(4,128)(2,1)S(1)}, bf16[1,4,10752]{2,1,0:T(4,128)(2,1)S(1)}, u32[]{:S(2)}, u32[]{:S(2)}) %collective-permute-start.16) | collective-permute-done | bytes 86048 | tf_op jit(solution)/shard_map/ppermute | solution.py:516
  19.8 0.0 collective-permute-done.17
  19.8 0.0 collective-permute-done.15
  19.8 9.9 %conditional.1 = ((bf16[1,4,10752]{2,1,0:T(4,128)(2,1)}, bf16[1,4,10752]{2,1,0:T(4,128)(2,1)})) conditional(s32[]{:T(128)} %bitcast.1, (s32[1]{0:T(128)}, f32[2,128]{1,0:T(2,128)S(1)}, bf16[1,4,10752]{2,1,0:T(4,128)(2,1)S(1)}, bf16[1,4,10752]{2,1,0:T(4,128)(2,1)S(1)}) %tuple.31, (bf16[1,4,10752]{2,1,0:T(4,128)(2,1)S(1)}, ...), branch_computations={%region_0.0_spmd, %region_1.0_spmd, %region_2.0_spmd, %region_3.0_... | conditional | flops 1073741824 | bytes 1032320 | solution.py:528
  19.8 3.1 %collective-permute-start.5 = (bf16[1,4,10752]{2,1,0:T(4,128)(2,1)S(1)}, bf16[1,4,10752]{2,1,0:T(4,128)(2,1)S(1)}, u32[]{:S(2)}, u32[]{:S(2)}) collective-permute-start(bf16[1,4,10752]{2,1,0:T(4,128)(2,1)S(1)} %get-tuple-element.118.refs_3_), channel_id=1, source_target_pairs={{0,12},{4,8},{8,4},{12,0},{1,13},{5,9},{9,5},{13,1},{2,14},{6,10},... | collective-permute-start | bytes 258056 | tf_op jit(solution)/shard_map/cond/branch_5_fun/ppermute | solution.py:516
  23.0 0.3 collective-permute-start.6
  23.3 3.8 %collective-permute-done.5.refs_4_ = bf16[1,4,10752]{2,1,0:T(4,128)(2,1)S(1)} collective-permute-done((bf16[1,4,10752]{2,1,0:T(4,128)(2,1)S(1)}, bf16[1,4,10752]{2,1,0:T(4,128)(2,1)S(1)}, u32[]{:S(2)}, u32[]{:S(2)}) %collective-permute-start.5) | collective-permute-done | bytes 86048 | tf_op jit(solution)/shard_map/cond/branch_5_fun/ppermute | solution.py:516
  27.0 1.2 %collective-permute-done.6.refs_5_ = bf16[1,4,10752]{2,1,0:T(4,128)(2,1)S(1)} collective-permute-done((bf16[1,4,10752]{2,1,0:T(4,128)(2,1)S(1)}, bf16[1,4,10752]{2,1,0:T(4,128)(2,1)S(1)}, u32[]{:S(2)}, u32[]{:S(2)}) %collective-permute-start.6) | collective-permute-done | bytes 86048 | tf_op jit(solution)/shard_map/cond/branch_5_fun/ppermute | solution.py:516
  28.3 1.4 %finish.13 = (bf16[1,4,10752]{2,1,0:T(4,128)(2,1)}, bf16[1,4,10752]{2,1,0:T(4,128)(2,1)}) custom-call(s32[1]{0:T(128)} %get-tuple-element.113.pick_ref, f32[2,128]{1,0:T(2,128)S(1)} %get-tuple-element.114.coef_ref, bf16[1,4,10752]{2,1,0:T(4,128)(2,1)S(1)} %get-tuple-element.115.refs_0_, bf16[1,4,10752]{2,1,0:T(4,128)(2,1)S(1)} %get-tuple-element.116.refs_1_, ...), custom_call_target="tpu_custom_call" | custom-call | flops 1073741824 | tf_op jit(solution)/shard_map/cond/branch_5_fun/finish/pallas_call | solution.py:402
  (2 shorter events, 0.0 us)
Async XLA Ops:
  1.3 12.2 %copy-start.1 = (f32[16,128]{1,0:T(8,128)S(1)}, f32[16,128]{1,0:T(8,128)}, u32[]{:S(2)}) copy-start(f32[16,128]{1,0:T(8,128)} %constant.17.clone.refs_3_.refs_8_.refs_11_) | copy-start | bytes 24580
  6.8 6.6 %copy-start = (f32[16,128]{1,0:T(8,128)S(1)}, f32[16,128]{1,0:T(8,128)}, u32[]{:S(2)}) copy-start(f32[16,128]{1,0:T(8,128)} %constant.16.clone.refs_2_.refs_7_.refs_10_) | copy-start | bytes 24580
  6.8 8.1 %collective-permute-start.12 = (bf16[512,256]{1,0:T(8,128)(2,1)S(1)}, bf16[512,256]{1,0:T(8,128)(2,1)S(1)}, u32[]{:S(2)}, u32[]{:S(2)}) collective-permute-start(bf16[512,256]{1,0:T(8,128)(2,1)S(1)} %get-tuple-element.157.own_ref), channel_id=1, source_target_pairs={{0,2},{1,3},{2,0},{3,1},{4,6},{5,7},{6,4},{7,5},{8,10},{9,11},{10,... | collective-permute-start | bytes 786440 | tf_op jit(solution)/shard_map/ppermute | solution.py:462
  8.4 6.6 %collective-permute-start.14 = (bf16[512,256]{1,0:T(8,128)(2,1)S(1)}, bf16[512,256]{1,0:T(8,128)(2,1)S(1)}, u32[]{:S(2)}, u32[]{:S(2)}) collective-permute-start(bf16[512,256]{1,0:T(8,128)(2,1)S(1)} %get-tuple-element.157.own_ref), channel_id=1, source_target_pairs={{0,1},{1,0},{2,3},{3,2},{4,5},{5,4},{6,7},{7,6},{8,9},{9,8},{10,11... | collective-permute-start | bytes 786440 | tf_op jit(solution)/shard_map/ppermute | solution.py:392
  8.4 11.4 %collective-permute-start.15 = (bf16[1,4,10752]{2,1,0:T(4,128)(2,1)S(1)}, bf16[1,4,10752]{2,1,0:T(4,128)(2,1)S(1)}, u32[]{:S(2)}, u32[]{:S(2)}) collective-permute-start(bf16[1,4,10752]{2,1,0:T(4,128)(2,1)S(1)} %get-tuple-element.156), channel_id=1, source_target_pairs={{0,4},{4,0},{8,12},{12,8},{1,5},{5,1},{9,13},{13,9},{2,6},{6,2},{1... | collective-permute-start | bytes 258056 | tf_op jit(solution)/shard_map/ppermute | solution.py:516
  10.0 9.9 %collective-permute-start.16 = (bf16[1,4,10752]{2,1,0:T(4,128)(2,1)S(1)}, bf16[1,4,10752]{2,1,0:T(4,128)(2,1)S(1)}, u32[]{:S(2)}, u32[]{:S(2)}) collective-permute-start(bf16[1,4,10752]{2,1,0:T(4,128)(2,1)S(1)} %get-tuple-element.156), channel_id=1, source_target_pairs={{0,8},{4,12},{8,0},{12,4},{1,9},{5,13},{9,1},{13,5},{2,10},{6,14},... | collective-permute-start | bytes 258056 | tf_op jit(solution)/shard_map/ppermute | solution.py:516
  12.6 7.3 %collective-permute-start.17 = (bf16[1,4,10752]{2,1,0:T(4,128)(2,1)S(1)}, bf16[1,4,10752]{2,1,0:T(4,128)(2,1)S(1)}, u32[]{:S(2)}, u32[]{:S(2)}) collective-permute-start(bf16[1,4,10752]{2,1,0:T(4,128)(2,1)S(1)} %get-tuple-element.156), channel_id=1, source_target_pairs={{0,12},{4,8},{8,4},{12,0},{1,13},{5,9},{9,5},{13,1},{2,14},{6,10},... | collective-permute-start | bytes 258056 | tf_op jit(solution)/shard_map/ppermute | solution.py:516
  14.9 1.6 %collective-permute-start.13 = (bf16[512,256]{1,0:T(8,128)(2,1)S(1)}, bf16[512,256]{1,0:T(8,128)(2,1)S(1)}, u32[]{:S(2)}, u32[]{:S(2)}) collective-permute-start(bf16[512,256]{1,0:T(8,128)(2,1)S(1)} %collective-permute-done.12.refs_1_), channel_id=1, source_target_pairs={{0,1},{1,0},{2,3},{3,2},{4,5},{5,4},{6,7},{7,6},{8,9},{9,8},{10,11... | collective-permute-start | bytes 786440 | tf_op jit(solution)/shard_map/ppermute | solution.py:392
  19.8 7.2 %collective-permute-start.5 = (bf16[1,4,10752]{2,1,0:T(4,128)(2,1)S(1)}, bf16[1,4,10752]{2,1,0:T(4,128)(2,1)S(1)}, u32[]{:S(2)}, u32[]{:S(2)}) collective-permute-start(bf16[1,4,10752]{2,1,0:T(4,128)(2,1)S(1)} %get-tuple-element.118.refs_3_), channel_id=1, source_target_pairs={{0,12},{4,8},{8,4},{12,0},{1,13},{5,9},{9,5},{13,1},{2,14},{6,10},... | collective-permute-start | bytes 258056 | tf_op jit(solution)/shard_map/cond/branch_5_fun/ppermute | solution.py:516
  23.0 5.3 %collective-permute-start.6 = (bf16[1,4,10752]{2,1,0:T(4,128)(2,1)S(1)}, bf16[1,4,10752]{2,1,0:T(4,128)(2,1)S(1)}, u32[]{:S(2)}, u32[]{:S(2)}) collective-permute-start(bf16[1,4,10752]{2,1,0:T(4,128)(2,1)S(1)} %get-tuple-element.118.refs_3_), channel_id=1, source_target_pairs={{0,4},{4,0},{8,12},{12,8},{1,5},{5,1},{9,13},{13,9},{2,6},{6,2},{1... | collective-permute-start | bytes 258056 | tf_op jit(solution)/shard_map/cond/branch_5_fun/ppermute | solution.py:516
